TPU v7x, 32 devices: a whole 2x2x4 slice. The times are simulated.
32 devices in a mesh: section: 4 (over y, core), gx: 8 (over z, x).
Axes of the slice: x: 2, y: 2, z: 4, core: 2. Of those that a mesh axis runs over, the one named last changes fastest.
Arguments:
- samples: bfloat16 [2, 1024, 32, 4096], P(None, 'gx', 'section'), may hold values from -8 to 8
- positions: float32 [2, 1024], replicated, may hold values from 0 to 8
- beam_dir: int32 [64], replicated, may hold values from 0 to 63, each once
- load_exp: int32 [4096], P(('section', 'gx')), may hold values from 0 to 3
Outputs:
- beams_out: bfloat16 [2, 64, 32, 4096], P(None, 'gx', 'section')
Inputs may be any that keep to these rules, and one draw needn't show every extreme that they name: `beam_dir`: every direction index 0 to 63 belongs to exactly one beam.
All inputs are finite; a program needn't handle non-finite values.
Results may differ from a plain program's by a relative error of at most 0.018.
Values may be sent and summed in bfloat16 or wider, within the bound.
A program may use at most 320 MiB of HBM per device.

v0:
```python
import math

import jax
import jax.numpy as jnp
from jax import lax
from jax.sharding import PartitionSpec as P

RADIX = 64
TAPS = 4
ITERS = 2


def from_behind(value, axis, steps):
    count = lax.axis_size(axis)
    initial, last = (max(0, -steps), min(count, count - steps))
    return lax.ppermute(value, axis, [(source, source + steps) for source in range(initial, last)])


def for_sending(x):
    return jax.tree.map(lambda a: a.astype(jnp.bfloat16) if a.dtype == jnp.float32 else a, x)


def prototype(taps_count, length):
    total_len = taps_count * length
    position = jnp.arange(total_len, dtype=jnp.int32).astype(jnp.float32) + 0.5
    window = 0.5 - 0.5 * jnp.cos(2.0 * math.pi / total_len * position)
    shaped = jnp.sinc((position - 0.5 * total_len) / length) * window
    return shaped.reshape(taps_count, length)


def dft_tables(radix_size):
    length = radix_size * radix_size
    counter = jnp.arange(radix_size, dtype=jnp.int32)
    products = counter[:, None] * counter[None, :]
    angles = 2.0 * math.pi / radix_size * (products % radix_size).astype(jnp.float32)
    twiddle = 2.0 * math.pi / length * products.astype(jnp.float32)
    return (
        jnp.cos(angles).astype(jnp.bfloat16),
        jnp.sin(angles).astype(jnp.bfloat16),
        jnp.cos(twiddle),
        jnp.sin(twiddle),
    )


def contract(matrix, values, pattern):
    return jnp.einsum(pattern, matrix, values, preferred_element_type=jnp.float32)


def transform(real_part, imag_part, direction_sign, radix_size):
    cosine, sine_table, twist_cos, twist_sin = dft_tables(radix_size)
    leading = real_part.shape[:-1]
    first_real = real_part.reshape(leading + (radix_size, radix_size))
    first_imag = imag_part.reshape(leading + (radix_size, radix_size))
    pattern_one = "fa,...ab->...fb"
    mid_real = contract(cosine, first_real, pattern_one) - direction_sign * contract(
        sine_table, first_imag, pattern_one
    )
    mid_imag = contract(cosine, first_imag, pattern_one) + direction_sign * contract(
        sine_table, first_real, pattern_one
    )
    turned_real = (mid_real * twist_cos - direction_sign * mid_imag * twist_sin).astype(
        jnp.bfloat16
    )
    turned_imag = (mid_imag * twist_cos + direction_sign * mid_real * twist_sin).astype(
        jnp.bfloat16
    )
    pattern_two = "gb,...fb->...gf"
    out_real = contract(cosine, turned_real, pattern_two) - direction_sign * contract(
        sine_table, turned_imag, pattern_two
    )
    out_imag = contract(cosine, turned_imag, pattern_two) + direction_sign * contract(
        sine_table, turned_real, pattern_two
    )
    inverse = 1.0 / radix_size
    full_shape = leading + (radix_size * radix_size,)
    return (
        (out_real * inverse).astype(jnp.bfloat16).reshape(full_shape),
        (out_imag * inverse).astype(jnp.bfloat16).reshape(full_shape),
    )


def beamform(spectra_block, loading, angular, projection):
    x_real = spectra_block[:, 0]
    x_imag = spectra_block[:, 1]
    snapshots = x_real.shape[1]
    inputs_all = x_real.shape[2]
    upper = jnp.concatenate([x_real, x_imag], axis=-1)
    lower = jnp.concatenate([-x_imag, x_real], axis=-1)
    blocked = jnp.concatenate([upper, lower], axis=1)
    phases = angular[:, None, None] * projection[None]
    steer = jnp.concatenate([jnp.cos(phases), -jnp.sin(phases)], axis=-1)
    solution = jnp.zeros_like(steer)
    residual = steer
    direction = steer
    residual_power = jnp.sum(residual * residual, axis=-1)
    load_col = loading[:, None]
    for sweep_index in range(ITERS):
        low_dir = direction.astype(jnp.bfloat16)
        proj = jnp.einsum(
            "jbm,jkm->jbk", low_dir, blocked, preferred_element_type=jnp.float32
        ).astype(jnp.bfloat16)
        low_wide = low_dir.astype(jnp.float32)
        image = (
            jnp.einsum("jbk,jkm->jbm", proj, blocked, preferred_element_type=jnp.float32)
            / snapshots
            + load_col[..., None] * low_wide
        )
        proj_wide = proj.astype(jnp.float32)
        curvature = jnp.sum(proj_wide * proj_wide, axis=-1) / snapshots + load_col * jnp.sum(
            low_wide * low_wide, axis=-1
        )
        step_size = (residual_power / curvature)[..., None]
        solution = solution + step_size * direction
        residual = residual - step_size * image
        new_power = jnp.sum(residual * residual, axis=-1)
        ratio = (new_power / residual_power)[..., None]
        direction = residual + ratio * direction
        residual_power = new_power
    mean_sq = jnp.sum(solution * solution, axis=-1) / inputs_all + 1e-06
    normalizer = lax.rsqrt(inputs_all * mean_sq)[..., None]
    weights = (solution * normalizer).astype(jnp.bfloat16)
    formed = jnp.einsum("jbm,jkm->jbk", weights, blocked, preferred_element_type=jnp.float32)
    output_real = formed[..., :snapshots].astype(jnp.bfloat16)
    output_imag = (-formed[..., snapshots:]).astype(jnp.bfloat16)
    return jnp.stack([output_real, output_imag], axis=1)


def body(samples, positions, beam_dir, load_exp):
    section_count = lax.axis_size("section")
    group_count = lax.axis_size("gx")
    inputs_dev = samples.shape[1]
    block_dev = samples.shape[2]
    length = samples.shape[3]
    chans_dev = load_exp.shape[0]
    history = TAPS - 1
    shaping = prototype(TAPS, length)
    earlier = from_behind(samples[:, :, block_dev - history :, :], "section", 1)
    extended = jnp.concatenate([earlier, samples], axis=2)
    filtered = shaping[0] * extended[:, :, history : history + block_dev, :].astype(jnp.float32)
    for tap_index in range(1, TAPS):
        filtered = filtered + shaping[tap_index] * extended[
            :, :, history - tap_index : history - tap_index + block_dev, :
        ].astype(jnp.float32)
    filtered = filtered.astype(jnp.bfloat16)
    spec_real, spec_imag = transform(filtered[0], filtered[1], -1.0, RADIX)
    spectra = jnp.stack([spec_real, spec_imag])
    sliced = spectra.reshape(2, inputs_dev, block_dev, section_count, group_count, chans_dev)
    packed = jnp.transpose(sliced, (0, 3, 4, 2, 1, 5)).reshape(
        2, section_count, group_count, block_dev * inputs_dev * chans_dev
    )
    turned = lax.all_to_all(
        lax.all_to_all(packed, "gx", split_axis=2, concat_axis=2, tiled=True),
        "section",
        split_axis=1,
        concat_axis=1,
        tiled=True,
    )
    unpacked = turned.reshape(2, section_count, group_count, block_dev, inputs_dev, chans_dev)
    channel_data = jnp.transpose(unpacked, (5, 0, 1, 3, 2, 4)).reshape(
        chans_dev, 2, section_count * block_dev, group_count * inputs_dev
    )
    first_channel = (
        lax.axis_index("section") * (length // section_count) + lax.axis_index("gx") * chans_dev
    )
    channel = first_channel + jnp.arange(chans_dev, dtype=jnp.int32)
    angular = 2.0 * math.pi * (0.75 + 0.5 * channel.astype(jnp.float32) / length)
    beam_total = beam_dir.shape[0]
    angle_beam = math.pi / beam_total * (beam_dir.astype(jnp.float32) + 0.5) - 0.5 * math.pi
    projection = (
        jnp.sin(angle_beam)[:, None] * positions[0][None, :]
        + jnp.cos(angle_beam)[:, None] * positions[1][None, :]
    )
    loading = jnp.exp2(load_exp.astype(jnp.float32))
    beam_spec = beamform(channel_data, loading, angular, projection)
    beam_dev = beam_total // group_count
    shaped = beam_spec.reshape(chans_dev, 2, group_count, beam_dev, section_count, block_dev)
    packed_back = jnp.transpose(shaped, (1, 2, 3, 4, 5, 0)).reshape(
        2, group_count, beam_dev, section_count, block_dev * chans_dev
    )
    returned = lax.all_to_all(
        lax.all_to_all(packed_back, "gx", split_axis=1, concat_axis=1, tiled=True),
        "section",
        split_axis=3,
        concat_axis=3,
        tiled=True,
    )
    opened = returned.reshape(2, group_count, beam_dev, section_count, block_dev, chans_dev)
    by_beam = jnp.transpose(opened, (0, 2, 4, 3, 1, 5)).reshape(2, beam_dev, block_dev, length)
    time_real, time_imag = transform(by_beam[0], by_beam[1], 1.0, RADIX)
    series = jnp.stack([time_real, time_imag]).astype(jnp.float32)
    margin_zeros = jnp.zeros((2, beam_dev, history, length), jnp.float32)
    padded = jnp.concatenate([margin_zeros, series, margin_zeros], axis=2)
    out_span = block_dev + history
    summed = shaping[TAPS - 1] * padded[:, :, history : history + out_span, :]
    for tap_index in range(1, TAPS):
        summed = (
            summed
            + shaping[TAPS - 1 - tap_index]
            * padded[:, :, history - tap_index : history - tap_index + out_span, :]
        )
    incoming = from_behind(for_sending(summed[:, :, block_dev:, :]), "section", 1)
    local_part = summed[:, :, :block_dev, :]
    carried = jnp.concatenate(
        [incoming, jnp.zeros((2, beam_dev, block_dev - history, length), jnp.float32)], axis=2
    )
    return (local_part + carried).astype(jnp.bfloat16)


def solution(mesh):
    placed = (P(None, "gx", "section", None), P(), P(), P(("section", "gx")))
    return jax.shard_map(
        body, mesh=mesh, in_specs=placed, out_specs=P(None, "gx", "section", None), check_vma=False
    )
```

profile of v0, /device:TPU:1, one launch (start us, length us, event | category | flops | bytes accessed | tf_op | source)
XLA Modules:
  0.0 1323.8 jit_solution(4472812272248343336)
XLA Ops:
  0.0 22.5 %copy.91 = bf16[2,128,8,4096]{1,3,2,0:T(8,128)(2,1)} copy(bf16[2,128,8,4096]{3,2,1,0:T(8,128)(2,1)} %param.4) | data formatting | bytes 33554432 | tf_op args[0]
  22.5 5.9 slice.121
  28.3 4.5 collective-permute-start
  33.7 67.4 %collective-permute-done = bf16[2,128,3,4096]{1,3,2,0:T(8,128)(2,1)} collective-permute-done((bf16[2,128,3,4096]{1,3,2,0:T(8,128)(2,1)}, bf16[2,128,3,4096]{1,3,2,0:T(8,128)(2,1)}, u32[]{:S(2)}, u32[]{:S(2)}) %collective-permute-start) | collective-permute-done | bytes 6291488 | tf_op jit(solution)/shard_map/ppermute | solution.py:16
  101.1 30.9 %add_convert_fusion = bf16[2,128,8,4096]{1,3,2,0:T(8,128)(2,1)} fusion(bf16[2,128,8,4096]{1,3,2,0:T(8,128)(2,1)} %copy.91, bf16[2,128,3,4096]{1,3,2,0:T(8,128)(2,1)} %collective-permute-done, f32[4096]{0:T(1024)S(1)} %get-tuple-element.26, f32[4096]{0:T(1024)S(1)} %get-tuple-element.24, f32[4096]{0:T(1024)S(1)} %get-tuple-element.25, ...), kind=kLoop, calls=%fused_computation.23 | loop fusion | flops 125829120 | bytes 39911424 | tf_op jit(solution)/shard_map/convert_element_type | solution.py:144
  132.0 7.0 fusion.160
  139.0 3.2 copy-done.2
  142.2 12.2 fusion.22
  154.4 12.2 fusion.26
  166.6 21.9 %multiply_subtract_fusion = f32[128,8,64,64]{0,3,2,1:T(8,128)} fusion(f32[128,8,64,64]{0,3,2,1:T(8,128)} %fusion.22, bf16[128,8,64,64]{0,3,2,1:T(8,128)(2,1)} %bitcast.136), kind=kOutput, calls=%fused_computation.43 | convolution fusion | flops 545320960 | bytes 41943040 | tf_op jit(solution)/shard_map/fa,...ab->...fb/dot_general | solution.py:46
  188.6 30.4 %fusion.13 = (bf16[128,8,64,64]{0,2,3,1:T(8,128)(2,1)S(1)}, bf16[128,8,64,64]{0,2,3,1:T(8,128)(2,1)}) fusion(f32[128,8,64,64]{0,3,2,1:T(8,128)} %multiply_subtract_fusion, f32[64,64]{0,1:T(8,128)S(1)} %copy.99, f32[64,64]{0,1:T(8,128)S(1)} %copy.96, f32[128,8,64,64]{0,3,2,1:T(8,128)} %fusion.26, bf16[128,8,64,64]{0,3,2,1:T(8,128)(2,1)} %bitcast.138), kind=kOutput, calls=%fused_computation.35 | convolution fusion | flops 578875392 | bytes 58753024 | tf_op jit(solution)/shard_map/fa,...ab->...fb/dot_general | solution.py:46
  219.0 4.2 copy-done.1
  223.3 12.4 fusion.19
  235.7 12.4 fusion.17
  248.0 21.4 %fusion.28 = bf16[128,8,64,64]{0,2,3,1:T(8,128)(2,1)} fusion(f32[128,8,64,64]{0,3,2,1:T(8,128)} %fusion.19, bf16[128,8,64,64]{0,2,3,1:T(8,128)(2,1)} %get-tuple-element.12), kind=kOutput, calls=%fused_computation.58 | convolution fusion | flops 553709568 | bytes 33554432 | tf_op jit(solution)/shard_map/gb,...fb->...gf/dot_general | solution.py:46
  269.4 12.0 copy.102
  281.4 21.1 %fusion.31 = bf16[128,8,64,64]{0,2,3,1:T(8,128)(2,1)} fusion(f32[128,8,64,64]{0,3,2,1:T(8,128)} %fusion.17, bf16[128,8,64,64]{0,2,3,1:T(8,128)(2,1)} %copy-done.1), kind=kOutput, calls=%fused_computation.59 | convolution fusion | flops 553709568 | bytes 33554432 | tf_op jit(solution)/shard_map/gb,...fb->...gf/dot_general | solution.py:46
  302.5 12.0 copy.105
  314.5 13.8 %maximum_bitcast_fusion = bf16[2,4,8,8,128,128]{4,5,2,1,3,0:T(8,128)(2,1)} fusion(bf16[1,128,8,4,8,128]{1,5,4,3,2,0:T(8,128)(2,1)} %bitcast.142, bf16[1,128,8,4,8,128]{1,5,4,3,2,0:T(8,128)(2,1)} %bitcast.141), kind=kLoop, calls=%fused_computation.31 | loop fusion | flops 8388608 | bytes 33554432 | tf_op jit(solution)/shard_map/transpose | solution.py:148
  328.3 21.6 %copy.141 = bf16[2,4,8,8,128,128]{5,4,3,1,0,2:T(8,128)(2,1)} copy(bf16[2,4,8,8,128,128]{4,5,2,1,3,0:T(8,128)(2,1)} %maximum_bitcast_fusion) | data formatting | bytes 33554432 | tf_op jit(solution)/shard_map/reshape | solution.py:148
  349.9 19.6 %reshape.200 = bf16[2,4,8,131072]{3,1,0,2:T(4,128)(2,1)} reshape(bf16[2,4,8,8,128,128]{5,4,3,1,0,2:T(8,128)(2,1)} %copy.141) | data formatting | bytes 33554432 | tf_op jit(solution)/shard_map/reshape | solution.py:148
  369.5 310.1 %all_to_all.20 = bf16[2,4,8,131072]{3,1,0,2:T(4,128)(2,1)S(1)} all-to-all(bf16[2,4,8,131072]{3,1,0,2:T(4,128)(2,1)} %reshape.200), channel_id=1, replica_groups=mesh['section'=4,'gx'=8] {'gx'}, dimensions={2} | all-to-all | bytes 33554432 | tf_op jit(solution)/shard_map/all_to_all | solution.py:152
  679.6 21.9 %copy.108 = bf16[2,4,8,131072]{3,2,0,1:T(8,128)(2,1)} copy(bf16[2,4,8,131072]{3,1,0,2:T(4,128)(2,1)S(1)} %all_to_all.20) | data formatting | bytes 33554432 | tf_op jit(solution)/shard_map/all_to_all | solution.py:152
  701.5 7.5 all-to-all-start.1
  709.3 120.1 %multiply_cosine_fusion = (f32[128,64,1024]{2,1,0:T(8,128)}, f32[128,64,1024]{2,1,0:T(8,128)}) fusion(f32[64,1024]{1,0:T(8,128)S(1)} %multiply_add_fusion.3, f32[128]{0:T(128)S(1)} %add_multiply_fusion), kind=kLoop, calls=%fused_computation.15 | loop fusion | flops 16777216 | bytes 67371520 | tf_op jit(solution)/shard_map/cos | solution.py:91
  829.4 20.9 %fusion = (f32[128,64]{1,0:T(8,128)S(1)}, f32[128,64]{1,0:T(8,128)S(1)}) fusion(f32[128,64,1024]{2,1,0:T(8,128)} %get-tuple-element.22, f32[128,64,1024]{2,1,0:T(8,128)} %get-tuple-element.21), kind=kLoop, calls=%fused_computation.2 | loop fusion | flops 117424128 | bytes 67174400 | tf_op jit(solution)/shard_map/reduce_sum | solution.py:109
  850.3 35.8 %all-to-all-done.1 = bf16[2,4,8,131072]{3,2,0,1:T(8,128)(2,1)} async-done(((bf16[2,4,8,131072]{3,2,0,1:T(8,128)(2,1)}), bf16[2,4,8,131072]{3,2,0,1:T(8,128)(2,1)}, u32[]{:S(2)}, u32[]{:S(2)}) %all-to-all-start.1) | async-done | bytes 16777248 | tf_op jit(solution)/shard_map/all_to_all | solution.py:151
  886.1 54.1 %copy.110 = bf16[128,2,4,8,8,128]{5,3,4,2,0,1:T(8,128)(2,1)} copy(bf16[128,2,4,8,8,128]{0,4,5,3,1,2:T(8,128)(2,1)} %bitcast.107) | data formatting | bytes 33554432 | tf_op jit(solution)/shard_map/transpose | solution.py:159
  940.2 12.5 slice_bitcast_fusion
  952.7 7.2 fusion.157
  959.9 35.6 %multiply_reduce_fusion.5 = (f32[128,64]{1,0:T(8,128)S(1)}, bf16[128,64,64]{1,2,0:T(8,128)(2,1)S(1)}) fusion(bf16[128,32,1024]{2,1,0:T(8,128)(2,1)} %get-tuple-element.14, bf16[128,32,1024]{2,1,0:T(8,128)(2,1)} %fusion.157, bf16[128,32,1024]{2,1,0:T(8,128)(2,1)} %get-tuple-element.13, f32[128,64,1024]{2,1,0:T(8,128)} %get-tuple-element.22, ...), kind=kOutput, calls=%fused_computation.67 | convolution fusion | flops 2350899200 | bytes 93356032 | tf_op jit(solution)/shard_map/jbm,jkm->jbk/dot_general | solution.py:99
  995.6 57.4 %multiply_reduce_fusion.2 = (f32[128,64]{1,0:T(8,128)S(1)}, f32[128,64,2048]{2,1,0:T(8,128)}) fusion(f32[128]{0:T(128)S(1)} %multiply_exponential_fusion, f32[128,64]{1,0:T(8,128)S(1)} %add_divide_fusion.1, f32[128,64,1024]{2,1,0:T(8,128)} %get-tuple-element.22, f32[128,64,1024]{2,1,0:T(8,128)} %get-tuple-element.21, ...), kind=kOutput, calls=%fused_computation.12 | convolution fusion | flops 2449465344 | bytes 160498176 | tf_op jit(solution)/shard_map/jbk,jkm->jbm/dot_general | solution.py:104
  1053.0 54.0 %multiply_reduce_fusion.1 = (f32[128,64]{1,0:T(8,128)S(1)}, bf16[128,64,2048]{2,1,0:T(8,128)(2,1)}) fusion(f32[128,64]{1,0:T(8,128)S(1)} %div.89, f32[128]{0:T(128)S(1)} %multiply_exponential_fusion, f32[128,64,2048]{2,1,0:T(8,128)} %get-tuple-element.34, f32[128,64]{1,0:T(8,128)S(1)} %add_divide_fusion.1, f32[128,64,1024]{2,1,0:T(8,128)} %get-tuple-element.22, ...), kind=kLoop, calls=%fused_computation.10 | loop fusion | flops 234872832 | bytes 167870976 | tf_op jit(solution)/shard_map/reduce_sum | solution.py:109
  1107.0 25.4 %multiply_reduce_fusion.4 = f32[128,64]{1,0:T(8,128)S(1)} fusion(bf16[128,64,2048]{2,1,0:T(8,128)(2,1)} %get-tuple-element.10, bf16[128,32,1024]{2,1,0:T(8,128)(2,1)} %get-tuple-element.14, bf16[128,32,1024]{2,1,0:T(8,128)(2,1)} %fusion.157, bf16[128,32,1024]{2,1,0:T(8,128)(2,1)} %get-tuple-element.13), kind=kOutput, calls=%fused_computation.66 | convolution fusion | flops 2283790336 | bytes 58753024 | tf_op jit(solution)/shard_map/jbm,jkm->jbk/dot_general | solution.py:99
  1132.5 67.5 %multiply_reduce_fusion = (f32[128,64]{1,0:T(8,128)S(1)}, f32[128,64,2048]{2,1,0:T(8,128)}) fusion(f32[128,64]{1,0:T(8,128)S(1)} %div.89, f32[128]{0:T(128)S(1)} %multiply_exponential_fusion, f32[128,64,2048]{2,1,0:T(8,128)} %get-tuple-element.34, f32[128,64]{1,0:T(8,128)S(1)} %add_divide_fusion, f32[128,64,1024]{2,1,0:T(8,128)} %get-tuple-element.22, ...), kind=kLoop, calls=%fused_computation.8 | loop fusion | flops 251650048 | bytes 201458176 | tf_op jit(solution)/shard_map/reduce_sum | solution.py:119
  1200.0 35.4 %fusion.5 = f32[128,64,64]{1,2,0:T(8,128)} fusion(f32[128,64,2048]{2,1,0:T(8,128)} %get-tuple-element.8, f32[128,64]{1,0:T(8,128)S(1)} %multiply_rsqrt_fusion, bf16[128,32,1024]{2,1,0:T(8,128)(2,1)} %get-tuple-element.14, bf16[128,32,1024]{2,1,0:T(8,128)(2,1)} %fusion.157, bf16[128,32,1024]{2,1,0:T(8,128)(2,1)} %get-tuple-element.13), kind=kOutput, calls=%fused_computation.17 | convolution fusion | flops 2315255808 | bytes 94404608 | tf_op jit(solution)/shard_map/jbm,jkm->jbk/dot_general | solution.py:122
  1235.4 1.8 slice.132
  1237.2 2.8 slice.174
  1241.8 2.8 copy.112
  1245.4 27.2 %all_to_all.21 = bf16[2,8,8,4,1024]{4,2,3,0,1:T(8,128)(2,1)S(1)} all-to-all(bf16[2,8,8,4,1024]{4,2,3,0,1:T(8,128)(2,1)S(1)} %copy.115), channel_id=1, replica_groups=mesh['section'=4,'gx'=8] {'gx'}, dimensions={1} | all-to-all | bytes 2097152 | tf_op jit(solution)/shard_map/all_to_all | solution.py:181
  1273.6 5.8 all-to-all-start.3
  1279.6 13.2 all-to-all-done.3
  1294.0 1.9 fusion.84
  1296.9 2.2 convolution_subtract_fusion
  1300.7 1.9 fusion.78
  1305.5 2.2 fusion.46
  1313.3 2.9 collective-permute-start.1
  1316.2 6.1 collective-permute-done.1
  (76 shorter events, 18.3 us)
Async XLA Ops:
  28.3 72.7 %collective-permute-start = (bf16[2,128,3,4096]{1,3,2,0:T(8,128)(2,1)}, bf16[2,128,3,4096]{1,3,2,0:T(8,128)(2,1)}, u32[]{:S(2)}, u32[]{:S(2)}) collective-permute-start(bf16[2,128,3,4096]{1,3,2,0:T(8,128)(2,1)} %slice.121), channel_id=1, source_target_pairs={{0,8},{8,16},{16,24},{1,9},{9,17},{17,25},{2,10},{10,18},{18,26},{... | collective-permute-start | bytes 18874376 | tf_op jit(solution)/shard_map/ppermute | solution.py:16
  33.1 155.5 %copy-start.3 = (f32[64,64]{0,1:T(8,128)}, f32[64,64]{0,1:T(8,128)S(1)}, u32[]{:S(2)}) copy-start(f32[64,64]{0,1:T(8,128)S(1)} %copy.96) | copy-start | bytes 49156
  33.7 98.3 %copy-start.5 = (f32[4096]{0:T(1024)}, f32[4096]{0:T(1024)S(1)}, u32[]{:S(2)}) copy-start(f32[4096]{0:T(1024)S(1)} %get-tuple-element.23) | copy-start | bytes 49156
  33.7 98.3 %copy-start.7 = (f32[4096]{0:T(1024)}, f32[4096]{0:T(1024)S(1)}, u32[]{:S(2)}) copy-start(f32[4096]{0:T(1024)S(1)} %get-tuple-element.24) | copy-start | bytes 49156
  33.7 98.3 %copy-start.9 = (f32[4096]{0:T(1024)}, f32[4096]{0:T(1024)S(1)}, u32[]{:S(2)}) copy-start(f32[4096]{0:T(1024)S(1)} %get-tuple-element.25) | copy-start | bytes 49156
  33.7 98.3 %copy-start.11 = (f32[4096]{0:T(1024)}, f32[4096]{0:T(1024)S(1)}, u32[]{:S(2)}) copy-start(f32[4096]{0:T(1024)S(1)} %get-tuple-element.26) | copy-start | bytes 49156
  138.9 3.2 copy-start.2
  138.9 15.5 %copy-start = (bf16[1,128,8,4096]{1,3,2,0:T(8,128)(2,1)}, bf16[1,128,8,4096]{1,3,2,0:T(8,128)(2,1)S(1)}, u32[]{:S(2)}) copy-start(bf16[1,128,8,4096]{1,3,2,0:T(8,128)(2,1)S(1)} %get-tuple-element.16) | copy-start | bytes 25165828
  219.0 4.3 copy-start.1
  219.0 16.6 %slice-start = ((s8[8388608]{0:T(1024)(128)(4,1)}), s8[4194304]{0:T(1024)(128)(4,1)S(1)}, s32[]{:S(2)}) async-start(s8[8388608]{0:T(1024)(128)(4,1)} %bitcast.139), calls=%async_computation.4 | async-start | bytes 8388608
  223.3 12.4 slice-start.1
  701.5 7.6 copy-start.14
  701.5 7.6 copy-start.15
  701.5 7.7 copy-start.13
  701.5 184.5 %all-to-all-start.1 = ((bf16[2,4,8,131072]{3,2,0,1:T(8,128)(2,1)}), bf16[2,4,8,131072]{3,2,0,1:T(8,128)(2,1)}, u32[]{:S(2)}, u32[]{:S(2)}) async-start(bf16[2,4,8,131072]{3,2,0,1:T(8,128)(2,1)} %copy.108), calls=%async_computation.1 | async-start | bytes 33554432 | tf_op jit(solution)/shard_map/all_to_all | solution.py:151
  1241.8 57.3 %copy-start.4 = (f32[64,64]{0,1:T(8,128)S(1)}, f32[64,64]{0,1:T(8,128)}, u32[]{:S(2)}) copy-start(f32[64,64]{0,1:T(8,128)} %copy-done.3) | copy-start | bytes 49156
  1273.6 19.2 %all-to-all-start.3 = ((bf16[2,8,8,4,1024]{4,2,1,0,3:T(8,128)(2,1)}), bf16[2,8,8,4,1024]{4,2,1,0,3:T(8,128)(2,1)S(1)}, u32[]{:S(2)}, u32[]{:S(2)}) async-start(bf16[2,8,8,4,1024]{4,2,1,0,3:T(8,128)(2,1)} %copy.116), calls=%async_computation.3 | async-start | bytes 2097152 | tf_op jit(solution)/shard_map/all_to_all | solution.py:180
  1300.1 11.1 copy-start.6
  1300.1 11.1 copy-start.8
  1300.1 11.1 copy-start.10
  1300.2 11.1 copy-start.12
  1313.3 9.0 collective-permute-start.1
where the time goes:
time: 1330 us; the launch traced here: 1320 us
  blocking collectives  337 us (25%)
  other arithmetic  320 us (24%)
  matrix products  309 us (23%)
  local copies, waits for them, and re-layouts  213 us (16%)
  waiting for transfers between devices  122 us (9%)
  starting transfers between devices  20.7 us (2%)
    all_to_all x1, blocking collectives, body(): lax.all_to_all(packed, 'gx', split_axis=2, concat_axis=2, tiled=True)  310 us
    dot_general x16, matrix products, contract(): jnp.einsum(pattern, matrix, values, preferred_element_type=jnp.float32)  155 us
    cos x1, other arithmetic, beamform(): steer = jnp.concatenate([jnp.cos(phases), -jnp.sin(phases)], axis=-1)  120 us
    reduce_sum x2, other arithmetic, beamform(): jnp.sum(low_wide * low_wide, axis=-1)  74.9 us
    ppermute x2, waiting for transfers between devices, from_behind(): lax.ppermute(value, axis, [(source, source + steps) for source in range(i...  73.5 us
    reduce_sum x1, other arithmetic, beamform(): mean_sq = jnp.sum(solution * solution, axis=-1) / inputs_all + 1e-06  67.5 us
    dot_general x2, matrix products, beamform(): jnp.einsum('jbm,jkm->jbk', low_dir, blocked, preferred_element_type=jnp.f...  61 us
    dot_general x1, matrix products, beamform(): jnp.einsum('jbk,jkm->jbm', proj, blocked, preferred_element_type=jnp.floa...  57.4 us
  transfers between devices with their start and end apart: 4, of which 4 were waited for; matrix products, arithmetic and copies ran while one was open for 11% of the time, Pallas kernels for 0%

commit v1 on v0

v1 whole, which is shorter than its diff:
```python
import math

import jax
import jax.numpy as jnp
from jax import lax
from jax.sharding import PartitionSpec as P

RADIX = 64
TAPS = 4
ITERS = 2
PIECES = 4


def from_behind(value, axis, steps):
    count = lax.axis_size(axis)
    initial, last = (max(0, -steps), min(count, count - steps))
    return lax.ppermute(value, axis, [(source, source + steps) for source in range(initial, last)])


def for_sending(x):
    return jax.tree.map(lambda a: a.astype(jnp.bfloat16) if a.dtype == jnp.float32 else a, x)


def prototype(taps_count, length):
    total_len = taps_count * length
    position = jnp.arange(total_len, dtype=jnp.int32).astype(jnp.float32) + 0.5
    window = 0.5 - 0.5 * jnp.cos(2.0 * math.pi / total_len * position)
    shaped = jnp.sinc((position - 0.5 * total_len) / length) * window
    return shaped.reshape(taps_count, length)


def dft_tables(radix_size):
    length = radix_size * radix_size
    counter = jnp.arange(radix_size, dtype=jnp.int32)
    products = counter[:, None] * counter[None, :]
    angles = 2.0 * math.pi / radix_size * (products % radix_size).astype(jnp.float32)
    twiddle = 2.0 * math.pi / length * products.astype(jnp.float32)
    return (
        jnp.cos(angles).astype(jnp.bfloat16),
        jnp.sin(angles).astype(jnp.bfloat16),
        jnp.cos(twiddle),
        jnp.sin(twiddle),
    )


def stacked_tables(direction_sign):
    cosine, sine_table, twist_cos, twist_sin = dft_tables(RADIX)
    signed = (direction_sign * sine_table.astype(jnp.float32)).astype(jnp.bfloat16)
    top = jnp.concatenate([cosine, -signed], axis=1)
    bottom = jnp.concatenate([signed, cosine], axis=1)
    return jnp.concatenate([top, bottom], axis=0), twist_cos, direction_sign * twist_sin


def halo_filter(samples):
    block_dev = samples.shape[2]
    history = TAPS - 1
    shaping = prototype(TAPS, samples.shape[3])
    earlier = from_behind(samples[:, :, block_dev - history :, :], "section", 1)
    extended = jnp.concatenate([earlier, samples], axis=2)
    filtered = shaping[0] * extended[:, :, history : history + block_dev, :].astype(jnp.float32)
    for tap_index in range(1, TAPS):
        filtered = filtered + shaping[tap_index] * extended[
            :, :, history - tap_index : history - tap_index + block_dev, :
        ].astype(jnp.float32)
    return filtered.astype(jnp.bfloat16)


def first_stage(filtered):
    _, inputs_dev, block_dev, _ = filtered.shape
    matrix, twist_cos, twist_sin = stacked_tables(-1.0)
    by_input = jnp.transpose(
        filtered.reshape(2, inputs_dev, block_dev, RADIX, RADIX), (2, 0, 3, 4, 1)
    ).reshape(block_dev, 2 * RADIX, RADIX * inputs_dev)
    mid = jnp.einsum("fi,kiz->kfz", matrix, by_input, preferred_element_type=jnp.float32)
    mid = mid.reshape(block_dev, 2, RADIX, RADIX, inputs_dev)
    cos_col, sin_col = twist_cos[..., None], twist_sin[..., None]
    real = (mid[:, 0] * cos_col - mid[:, 1] * sin_col).astype(jnp.bfloat16)
    imag = (mid[:, 1] * cos_col + mid[:, 0] * sin_col).astype(jnp.bfloat16)
    return jnp.concatenate([real, imag], axis=2)


def second_stage(turned):
    matrix, _, _ = stacked_tables(-1.0)
    out = jnp.einsum("gl,kalm->kagm", matrix, turned, preferred_element_type=jnp.float32)
    return (out * (1.0 / RADIX)).astype(jnp.bfloat16)


def rotation(scale, delay):
    phase = scale[:, None, None] * delay[None]
    return jnp.cos(phase), -jnp.sin(phase)


def local_products(spectra, steer):
    chans, _, snapshots, _ = spectra.shape
    x_real, x_imag = spectra[:, 0], spectra[:, 1]
    upper = jnp.concatenate([x_real, x_imag], axis=-1)
    lower = jnp.concatenate([-x_imag, x_real], axis=-1)
    blocked = jnp.concatenate([upper, lower], axis=1)
    projected = jnp.einsum("fbm,fkm->fbk", steer, blocked, preferred_element_type=jnp.float32)
    gram = jnp.einsum("fqm,fkm->fqk", upper, blocked, preferred_element_type=jnp.float32)
    row = jnp.arange(snapshots)[:, None]
    col = jnp.arange(snapshots)[None, :]
    packed = jnp.where(row <= col, gram[..., :snapshots], gram[..., snapshots:])
    return projected.astype(jnp.bfloat16), packed


def solve(projected, packed, loading, inputs_all):
    snapshots = packed.shape[-1]
    row = jnp.arange(snapshots)[:, None]
    col = jnp.arange(snapshots)[None, :]
    flipped = jnp.swapaxes(packed, 1, 2)
    gram_real = jnp.where(row <= col, packed, flipped)
    gram_imag = jnp.where(row < col, -flipped, jnp.where(row > col, packed, 0.0))
    gram = jnp.concatenate(
        [
            jnp.concatenate([gram_real, gram_imag], axis=2),
            jnp.concatenate([-gram_imag, gram_real], axis=2),
        ],
        axis=1,
    )
    y = projected.astype(jnp.float32)
    v = jnp.einsum("fbq,fqk->fbk", y, gram, precision=lax.Precision.HIGHEST)
    load = loading[:, None]
    n1 = jnp.sum(y * y, axis=-1)
    n2 = jnp.sum(y * v, axis=-1)
    spread = n2 - n1 * n1 / inputs_all
    curv_first = n1 / snapshots + load * inputs_all
    alpha_first = inputs_all / curv_first
    h = alpha_first / snapshots
    power = h * h * spread
    beta = power / inputs_all
    along = h * n1 / inputs_all + beta
    second = along[..., None] * y - h[..., None] * v
    curv_second = jnp.sum(second * second, axis=-1) / snapshots + load * (
        power + beta * beta * inputs_all
    )
    alpha_second = power / curv_second
    on_steer = alpha_first + alpha_second * along
    on_image = -alpha_second * h
    lean = on_steer + on_image * n1 / inputs_all
    mean_sq = (lean * lean * inputs_all + on_image * on_image * spread) / inputs_all + 1e-06
    normalizer = lax.rsqrt(inputs_all * mean_sq)
    formed = (normalizer * on_steer)[..., None] * y + (normalizer * on_image)[..., None] * v
    return jnp.stack(
        [formed[..., :snapshots], -formed[..., snapshots:]], axis=0
    ).astype(jnp.bfloat16)


def synthesis_transform(values):
    matrix, twist_cos, twist_sin = stacked_tables(1.0)
    _, beams, blocks, _, _ = values.shape
    rows = beams * blocks
    z = jnp.transpose(values.reshape(2, rows, RADIX, RADIX), (0, 3, 1, 2)).reshape(
        2 * RADIX, rows * RADIX
    )
    mid = jnp.einsum("fi,iz->fz", matrix, z, preferred_element_type=jnp.float32)
    mid = mid.reshape(2, RADIX, rows, RADIX)
    cos_col, sin_col = twist_cos[:, None, :], twist_sin[:, None, :]
    real = (mid[0] * cos_col - mid[1] * sin_col).astype(jnp.bfloat16)
    imag = (mid[1] * cos_col + mid[0] * sin_col).astype(jnp.bfloat16)
    turned = jnp.concatenate([real, imag], axis=2)
    out = jnp.einsum("gl,arl->rga", matrix, turned, preferred_element_type=jnp.float32)
    out = (out * (1.0 / RADIX)).astype(jnp.bfloat16).reshape(
        beams, blocks, 2, RADIX * RADIX
    )
    return jnp.transpose(out, (2, 0, 1, 3))


def body(samples, positions, beam_dir, load_exp):
    section_count = lax.axis_size("section")
    group_count = lax.axis_size("gx")
    section = lax.axis_index("section")
    group = lax.axis_index("gx")
    inputs_dev = samples.shape[1]
    inputs_all = positions.shape[1]
    block_dev = samples.shape[2]
    snapshots = block_dev * section_count
    length = samples.shape[3]
    history = TAPS - 1
    shaping = prototype(TAPS, length)
    beam_total = beam_dir.shape[0]
    beam_dev = beam_total // group_count
    rows_dev = RADIX // section_count
    rows_piece = rows_dev // PIECES
    chans_own = rows_piece * RADIX // group_count

    loading = jnp.exp2(load_exp.astype(jnp.float32))
    loading = lax.all_gather(loading, ("section", "gx"), tiled=True)
    loading = jnp.transpose(loading.reshape(RADIX, RADIX))
    loading = lax.dynamic_slice_in_dim(loading, section * rows_dev, rows_dev, 0)
    loading = loading.reshape(PIECES, group_count, chans_own)
    loading = lax.dynamic_index_in_dim(loading, group, 1, keepdims=False)

    angle_beam = math.pi / beam_total * (beam_dir.astype(jnp.float32) + 0.5) - 0.5 * math.pi
    mine = lax.dynamic_slice_in_dim(positions, group * inputs_dev, inputs_dev, 1)
    delay = (
        jnp.sin(angle_beam)[:, None] * mine[0][None, :]
        + jnp.cos(angle_beam)[:, None] * mine[1][None, :]
    )
    rows = (section * rows_dev + jnp.arange(rows_dev, dtype=jnp.int32)).astype(jnp.float32)
    low_cos, low_sin = rotation(2.0 * math.pi * (0.75 + 0.5 * rows / length), delay)
    steps = jnp.arange(RADIX, dtype=jnp.int32).astype(jnp.float32)
    high_cos, high_sin = rotation(math.pi * RADIX / length * steps, delay)

    turned = first_stage(halo_filter(samples))
    turned = turned.reshape(
        block_dev, section_count, rows_dev, 2 * RADIX, inputs_dev
    )
    formed = []
    for piece in range(PIECES):
        span = slice(piece * rows_piece, (piece + 1) * rows_piece)
        part = turned[:, :, span].reshape(
            block_dev, section_count * rows_piece, 2 * RADIX, inputs_dev
        )
        spectra = second_stage(part).reshape(
            block_dev, section_count, rows_piece, 2, RADIX, inputs_dev
        )
        spectra = jnp.transpose(spectra, (1, 0, 2, 3, 4, 5))
        spectra = lax.all_to_all(spectra, "section", split_axis=0, concat_axis=0, tiled=True)
        spectra = spectra.reshape(snapshots, rows_piece, 2, RADIX, inputs_dev)
        spectra = jnp.transpose(spectra, (1, 3, 2, 0, 4)).reshape(
            rows_piece * RADIX, 2, snapshots, inputs_dev
        )
        lc, ls = low_cos[span][:, None], low_sin[span][:, None]
        steer = jnp.concatenate(
            [lc * high_cos - ls * high_sin, lc * high_sin + ls * high_cos], axis=-1
        ).astype(jnp.bfloat16)
        steer = steer.reshape(rows_piece * RADIX, beam_total, 2 * inputs_dev)
        projected, packed = local_products(spectra, steer)
        projected = lax.psum_scatter(projected, "gx", scatter_dimension=0, tiled=True)
        packed = lax.psum_scatter(packed, "gx", scatter_dimension=0, tiled=True)
        formed.append(solve(projected, packed, loading[piece], inputs_all))

    beam_spec = jnp.stack(formed, axis=1)
    shaped = beam_spec.reshape(
        2, PIECES, chans_own, group_count, beam_dev, section_count, block_dev
    )
    packed_back = jnp.transpose(shaped, (0, 3, 4, 5, 6, 1, 2)).reshape(
        2, group_count, beam_dev, section_count, block_dev * PIECES * chans_own
    )
    returned = lax.all_to_all(
        lax.all_to_all(packed_back, "gx", split_axis=1, concat_axis=1, tiled=True),
        "section",
        split_axis=3,
        concat_axis=3,
        tiled=True,
    )
    opened = returned.reshape(
        2, group_count, beam_dev, section_count, block_dev, PIECES, chans_own
    )
    by_beam = jnp.transpose(opened, (0, 2, 4, 3, 5, 1, 6)).reshape(
        2, beam_dev, block_dev, RADIX, RADIX
    )
    series = synthesis_transform(by_beam).astype(jnp.float32)
    margin_zeros = jnp.zeros((2, beam_dev, history, length), jnp.float32)
    padded = jnp.concatenate([margin_zeros, series, margin_zeros], axis=2)
    out_span = block_dev + history
    summed = shaping[TAPS - 1] * padded[:, :, history : history + out_span, :]
    for tap_index in range(1, TAPS):
        summed = (
            summed
            + shaping[TAPS - 1 - tap_index]
            * padded[:, :, history - tap_index : history - tap_index + out_span, :]
        )
    incoming = from_behind(for_sending(summed[:, :, block_dev:, :]), "section", 1)
    local_part = summed[:, :, :block_dev, :]
    carried = jnp.concatenate(
        [incoming, jnp.zeros((2, beam_dev, block_dev - history, length), jnp.float32)], axis=2
    )
    return (local_part + carried).astype(jnp.bfloat16)


def solution(mesh):
    placed = (P(None, "gx", "section", None), P(), P(), P(("section", "gx")))
    return jax.shard_map(
        body, mesh=mesh, in_specs=placed, out_specs=P(None, "gx", "section", None), check_vma=False
    )
```

time: 1330 us -> 1390 us (1.045)
  waiting for transfers between devices: 122 us -> 770 us
  blocking collectives: 337 us -> 90.4 us
  matrix products: 309 us -> 97.3 us
  other arithmetic: 320 us -> 115 us
  local copies, waits for them, and re-layouts: 213 us -> 262 us
  starting transfers between devices: 20.7 us -> 37.1 us
  between operations: 0.78 us -> 14.7 us
    reduce_scatter x0 -> x8, waiting for transfers between devices: none -> 541 us  [the longest x4 344 us: body(): lax.psum_scatter(projected, 'gx', scatter_dimension=0, tiled=True)]
    all_to_all x1 -> x0, blocking collectives: 310 us -> none  [body(): lax.all_to_all(packed, 'gx', split_axis=2, concat_axis=2, tiled=True)]
    dot_general x20 -> x19, matrix products: 309 us -> 97.3 us  [the longest x4 32.6 us: local_products(): jnp.einsum('fbm,fkm->fbk', steer, blocked, preferred_element_type=jnp.flo...]
    reduce_sum x3 -> x4, other arithmetic: 142 us -> 5.53 us  [solve(): jnp.sum(second * second, axis=-1) / snapshots]
    cos x1 -> x2, other arithmetic: 120 us -> 10.7 us  [rotation(): return (jnp.cos(phase), -jnp.sin(phase))]
    all_to_all x1 -> x4, waiting for transfers between devices: 35.8 us -> 141 us  [body(): lax.all_to_all(spectra, 'section', split_axis=0, concat_axis=0, tiled=True)]
    all_gather x0 -> x1, blocking collectives: none -> 61.7 us  [body(): loading = lax.all_gather(loading, ('section', 'gx'), tiled=True)]
    reshape x5 -> x12, local copies, waits for them, and re-layouts: 42.5 us -> 70.5 us  [the longest x1 25.3 us: first_stage(): by_input = jnp.transpose(filtered.reshape(2, inputs_dev, block_dev, RADIX...]
  transfers between devices with their start and end apart: 4 -> 15, of which waited for: 4 -> 14; matrix products, arithmetic and copies ran while one was open for 11% -> 12% of each run, Pallas kernels for 0% -> 0%
where the time goes in v1:
time: 1390 us
  waiting for transfers between devices  770 us (55%)
  local copies, waits for them, and re-layouts  262 us (19%)
  other arithmetic  115 us (8%)
  matrix products  97.3 us (7%)
  blocking collectives  90.4 us (7%)
  starting transfers between devices  37.1 us (3%)
  between operations  14.7 us (1%)
    reduce_scatter x4, waiting for transfers between devices, body(): lax.psum_scatter(projected, 'gx', scatter_dimension=0, tiled=True)  344 us
    reduce_scatter x4, waiting for transfers between devices, body(): packed = lax.psum_scatter(packed, 'gx', scatter_dimension=0, tiled=True)  197 us
    all_to_all x4, waiting for transfers between devices, body(): lax.all_to_all(spectra, 'section', split_axis=0, concat_axis=0, tiled=True)  141 us
    ppermute x2, waiting for transfers between devices, from_behind(): lax.ppermute(value, axis, [(source, source + steps) for source in range(i...  73.1 us
    all_gather x1, blocking collectives, body(): loading = lax.all_gather(loading, ('section', 'gx'), tiled=True)  61.7 us
    unnamed x81, local copies, waits for them, and re-layouts  59.6 us
    dot_general x4, matrix products, local_products(): jnp.einsum('fbm,fkm->fbk', steer, blocked, preferred_element_type=jnp.flo...  32.6 us
    transpose x1, local copies, waits for them, and re-layouts, first_stage(): jnp.einsum('fi,kiz->kfz', matrix, by_input, preferred_element_type=jnp.fl...  31.1 us
  transfers between devices with their start and end apart: 15, of which 14 were waited for; matrix products, arithmetic and copies ran while one was open for 12% of the time, Pallas kernels for 0%

profile of v1, /device:TPU:1, one launch (start us, length us, event | category | flops | bytes accessed | tf_op | source)
XLA Modules:
  0.0 1385.8 jit_solution(8606752449608251764)
XLA Ops:
  6.5 22.5 %copy.180 = bf16[2,128,8,4096]{1,3,2,0:T(8,128)(2,1)} copy(bf16[2,128,8,4096]{3,2,1,0:T(8,128)(2,1)} %param.5) | data formatting | bytes 33554432 | tf_op args[0]
  37.6 67.0 %collective-permute-done = bf16[2,128,3,4096]{1,3,2,0:T(8,128)(2,1)S(1)} collective-permute-done((bf16[2,128,3,4096]{1,3,2,0:T(8,128)(2,1)S(1)}, bf16[2,128,3,4096]{1,3,2,0:T(8,128)(2,1)S(1)}, u32[]{:S(2)}, u32[]{:S(2)}) %collective-permute-start) | collective-permute-done | bytes 6291488 | tf_op jit(solution)/shard_map/ppermute | solution.py:17
  104.6 20.6 %add_convert_fusion = bf16[2,128,8,4096]{1,3,2,0:T(8,128)(2,1)S(1)} fusion(bf16[2,128,8,4096]{1,3,2,0:T(8,128)(2,1)} %copy.180, bf16[2,128,3,4096]{1,3,2,0:T(8,128)(2,1)S(1)} %collective-permute-done, f32[4096]{0:T(1024)S(1)} %get-tuple-element.79, f32[4096]{0:T(1024)S(1)} %get-tuple-element.77, f32[4096]{0:T(1024)S(1)} %get-tuple-element.78, ...), kind=kLoop, calls=%fused_computation | loop fusion | flops 125829120 | bytes 39911424 | tf_op jit(solution)/shard_map/convert_element_type | solution.py:65
  125.2 6.8 copy.183
  132.0 25.3 %reshape.1127 = bf16[8,128,8192]{2,1,0:T(8,128)(2,1)} reshape(bf16[8,2,64,64,128]{4,3,2,1,0:T(8,128)(2,1)} %copy.183) | data formatting | bytes 33554432 | tf_op jit(solution)/shard_map/reshape | solution.py:73
  157.3 16.6 %convolution_bitcast_fusion = f32[8,128,8192]{1,2,0:T(8,128)} fusion(bf16[8,128,8192]{2,1,0:T(8,128)(2,1)} %reshape.1127, bf16[64,64]{1,0:T(8,128)(2,1)S(1)} %get-tuple-element.126, bf16[64,64]{1,0:T(8,128)(2,1)S(1)} %get-tuple-element.125, bf16[64,64]{1,0:T(8,128)(2,1)S(1)} %fusion.157), kind=kOutput, calls=%fused_computation.11 | convolution fusion | flops 2147614720 | bytes 50356224 | tf_op jit(solution)/shard_map/fi,kiz->kfz/dot_general | solution.py:74
  173.9 31.1 %copy.185 = f32[8,128,8192]{2,1,0:T(8,128)} copy(f32[8,128,8192]{1,2,0:T(8,128)} %convolution_bitcast_fusion) | data formatting | bytes 67108864 | tf_op jit(solution)/shard_map/fi,kiz->kfz/transpose | solution.py:74
  205.0 27.6 %copy.280 = f32[128,8,64,128]{3,2,1,0:T(8,128)} copy(f32[128,8,64,128]{3,1,2,0:T(8,128)} %bitcast.190) | data formatting | bytes 67108864
  232.6 17.0 %fusion.205 = (f32[8,1,64,64,128]{4,3,2,1,0:T(8,128)S(1)}, f32[8,1,64,64,128]{4,3,2,1,0:T(8,128)}) fusion(f32[8,2,64,64,128]{4,3,2,1,0:T(8,128)} %bitcast.189), kind=kLoop, calls=%fused_computation.360 | loop fusion | bytes 67108864 | tf_op jit(solution)/shard_map/slice | solution.py:77
  249.6 14.1 %subtract_convert_fusion = (bf16[8,4,16,64,128]{4,3,2,1,0:T(8,128)(2,1)}, bf16[8,4,16,64,128]{4,3,2,1,0:T(8,128)(2,1)}) fusion(f32[8,4,16,64,128]{4,3,2,1,0:T(8,128)S(1)} %bitcast.192, f32[8,4,16,64,128]{4,3,2,1,0:T(8,128)} %bitcast.193, f32[4,16,64]{2,1,0:T(8,128)S(1)} %get-tuple-element.116, f32[4,16,64]{2,1,0:T(8,128)S(1)} %get-tuple-element.115), kind=kLoop, calls=%fused_computation.16 | loop fusion | flops 33554432 | bytes 50364416 | tf_op jit(solution)/shard_map/convert_element_type | solution.py:77
  263.6 10.2 fusion.19
  278.2 5.0 all-to-all-start
  289.6 38.8 %all-to-all-done = bf16[4,8,4,2,64,128]{5,4,3,2,1,0:T(8,128)(2,1)} async-done(((bf16[4,8,4,2,64,128]{5,4,3,2,1,0:T(8,128)(2,1)}), bf16[4,8,4,2,64,128]{5,4,3,2,1,0:T(8,128)(2,1)}, u32[]{:S(2)}, u32[]{:S(2)}) %all-to-all-start) | async-done | bytes 4194336 | tf_op jit(solution)/shard_map/all_to_all | solution.py:219
  328.5 7.1 all-to-all-start.3
  342.1 40.9 %all-to-all-done.3 = bf16[4,8,4,2,64,128]{5,4,3,2,1,0:T(8,128)(2,1)} async-done(((bf16[4,8,4,2,64,128]{5,4,3,2,1,0:T(8,128)(2,1)}), bf16[4,8,4,2,64,128]{5,4,3,2,1,0:T(8,128)(2,1)}, u32[]{:S(2)}, u32[]{:S(2)}) %all-to-all-start.3) | async-done | bytes 4194336 | tf_op jit(solution)/shard_map/all_to_all | solution.py:219
  383.0 5.7 all-to-all-start.2
  395.1 41.0 %all-to-all-done.2 = bf16[4,8,4,2,64,128]{5,4,3,2,1,0:T(8,128)(2,1)} async-done(((bf16[4,8,4,2,64,128]{5,4,3,2,1,0:T(8,128)(2,1)}), bf16[4,8,4,2,64,128]{5,4,3,2,1,0:T(8,128)(2,1)}, u32[]{:S(2)}, u32[]{:S(2)}) %all-to-all-start.2) | async-done | bytes 4194336 | tf_op jit(solution)/shard_map/all_to_all | solution.py:219
  436.1 5.7 all-to-all-start.1
  442.3 4.9 copy.187
  447.2 4.9 copy.224
  452.1 4.9 copy.211
  468.7 20.5 %all-to-all-done.1 = bf16[4,8,4,2,64,128]{5,4,3,2,1,0:T(8,128)(2,1)} async-done(((bf16[4,8,4,2,64,128]{5,4,3,2,1,0:T(8,128)(2,1)}), bf16[4,8,4,2,64,128]{5,4,3,2,1,0:T(8,128)(2,1)}, u32[]{:S(2)}, u32[]{:S(2)}) %all-to-all-start.1) | async-done | bytes 4194336 | tf_op jit(solution)/shard_map/all_to_all | solution.py:219
  489.2 5.1 copy.200
  506.5 6.7 fusion.36
  513.1 8.7 fusion.32
  529.6 12.0 slice_select_fusion.2
  544.8 8.8 multiply_cosine_fusion
  553.7 15.8 %subtract_convert_fusion.4 = (bf16[4,64,64,128]{3,2,1,0:T(8,128)(2,1)S(1)}, bf16[4,64,64,128]{3,2,1,0:T(8,128)(2,1)}, bf16[4,64,64,128]{3,2,1,0:T(8,128)(2,1)}, ...) fusion(f32[64,64,128]{2,1,0:T(8,128)} %get-tuple-element.89, ...), kind=kLoop, calls=%fused_computation.48 | loop fusion | flops 67108864 | bytes 38797312 | tf_op jit(solution)/shard_map/convert.41
  569.5 7.4 fusion.49
  578.4 8.3 fusion.46
  588.4 8.2 fusion.43
  597.2 61.7 %all-gather = f32[32,1,128]{2,1,0:T(1,128)S(1)} all-gather(f32[1,1,128]{2,1,0:T(1,128)S(1)} %exponential_bitcast_fusion), channel_id=1, replica_groups=mesh['section'=4,'gx'=8] {'section','gx'}, dimensions={0}, use_global_device_ids=true | all-gather | bytes 16896 | tf_op jit(solution)/shard_map/all_gather | solution.py:188
  660.4 8.7 fusion.40
  670.6 16.6 %reduce-scatter.23.cloned.1.call-done = f32[32,32,32]{1,2,0:T(8,128)} async-done(((f32[256,32,32]{1,2,0:T(8,128)}), f32[32,32,32]{1,2,0:T(8,128)}) %reduce-scatter.23.cloned.1.call-update) | async-done | bytes 131088 | tf_op jit(solution)/shard_map/reduce_scatter | solution.py:231
  688.5 90.0 %reduce-scatter.19.cloned.1.call-done = f32[32,32,32]{1,2,0:T(8,128)} async-done(((f32[256,32,32]{1,2,0:T(8,128)}), f32[32,32,32]{1,2,0:T(8,128)}) %reduce-scatter.19.cloned.1.call-update) | async-done | bytes 131088 | tf_op jit(solution)/shard_map/reduce_scatter | solution.py:231
  779.8 90.5 %reduce-scatter.15.cloned.1.call-done = f32[32,32,32]{1,2,0:T(8,128)} async-done(((f32[256,32,32]{1,2,0:T(8,128)}), f32[32,32,32]{1,2,0:T(8,128)}) %reduce-scatter.15.cloned.1.call-update) | async-done | bytes 131088 | tf_op jit(solution)/shard_map/reduce_scatter | solution.py:231
  877.2 84.4 %reduce-scatter.9.cloned.1.call-done = bf16[32,64,64]{1,2,0:T(8,128)(2,1)} async-done(((bf16[256,64,64]{1,2,0:T(8,128)(2,1)}), bf16[32,64,64]{1,2,0:T(8,128)(2,1)}) %reduce-scatter.9.cloned.1.call-update) | async-done | bytes 262160 | tf_op jit(solution)/shard_map/reduce_scatter | solution.py:230
  966.8 86.5 %reduce-scatter.13.cloned.1.call-done = bf16[32,64,64]{1,2,0:T(8,128)(2,1)} async-done(((bf16[256,64,64]{1,2,0:T(8,128)(2,1)}), bf16[32,64,64]{1,2,0:T(8,128)(2,1)}) %reduce-scatter.13.cloned.1.call-update) | async-done | bytes 262160 | tf_op jit(solution)/shard_map/reduce_scatter | solution.py:230
  1057.6 87.2 %reduce-scatter.17.cloned.1.call-done = bf16[32,64,64]{1,2,0:T(8,128)(2,1)} async-done(((bf16[256,64,64]{1,2,0:T(8,128)(2,1)}), bf16[32,64,64]{1,2,0:T(8,128)(2,1)}) %reduce-scatter.17.cloned.1.call-update) | async-done | bytes 262160 | tf_op jit(solution)/shard_map/reduce_scatter | solution.py:230
  1150.6 86.1 %reduce-scatter.21.cloned.1.call-done = bf16[32,64,64]{1,2,0:T(8,128)(2,1)} async-done(((bf16[256,64,64]{1,2,0:T(8,128)(2,1)}), bf16[32,64,64]{1,2,0:T(8,128)(2,1)}) %reduce-scatter.21.cloned.1.call-update) | async-done | bytes 262160 | tf_op jit(solution)/shard_map/reduce_scatter | solution.py:230
  1258.2 7.8 copy.260
  1266.0 8.7 reshape.1128
  1274.7 28.7 %all_to_all.30 = bf16[2,8,8,4,1024]{4,2,3,0,1:T(8,128)(2,1)S(1)} all-to-all(bf16[2,8,8,4,1024]{4,2,3,0,1:T(8,128)(2,1)S(1)} %reshape.1128), channel_id=1, replica_groups=mesh['section'=4,'gx'=8] {'gx'}, dimensions={1} | all-to-all | bytes 2097152 | tf_op jit(solution)/shard_map/all_to_all | solution.py:242
  1304.5 5.4 all-to-all-start.5
  1310.4 13.2 all-to-all-done.5
  1327.9 9.1 copy.287
  1337.0 5.0 reshape_reshape.3
  1371.3 6.1 collective-permute-done.1
  (206 shorter events, 156.2 us)
Async XLA Ops:
  6.5 536.1 %copy-start = (f32[2,1024]{1,0:T(2,128)S(1)}, f32[2,1024]{1,0:T(2,128)}, u32[]{:S(2)}) copy-start(f32[2,1024]{1,0:T(2,128)} %param.6) | copy-start | bytes 24580
  32.2 72.4 %collective-permute-start = (bf16[2,128,3,4096]{1,3,2,0:T(8,128)(2,1)S(1)}, bf16[2,128,3,4096]{1,3,2,0:T(8,128)(2,1)S(1)}, u32[]{:S(2)}, u32[]{:S(2)}) collective-permute-start(bf16[2,128,3,4096]{1,3,2,0:T(8,128)(2,1)S(1)} %slice.278), channel_id=1, source_target_pairs={{0,8},{8,16},{16,24},{1,9},{9,17},{17,25},{2,10},{10,18},{18,26},{... | collective-permute-start | bytes 18874376 | tf_op jit(solution)/shard_map/ppermute | solution.py:17
  37.1 351.6 %copy-start.22 = (bf16[64,64]{1,0:T(8,128)(2,1)}, bf16[64,64]{1,0:T(8,128)(2,1)S(1)}, u32[]{:S(2)}) copy-start(bf16[64,64]{1,0:T(8,128)(2,1)S(1)} %get-tuple-element.126) | copy-start | bytes 24580
  37.6 87.6 %copy-start.28 = (f32[4096]{0:T(1024)}, f32[4096]{0:T(1024)S(1)}, u32[]{:S(2)}) copy-start(f32[4096]{0:T(1024)S(1)} %get-tuple-element.76) | copy-start | bytes 49156
  37.6 87.6 %copy-start.30 = (f32[4096]{0:T(1024)}, f32[4096]{0:T(1024)S(1)}, u32[]{:S(2)}) copy-start(f32[4096]{0:T(1024)S(1)} %get-tuple-element.77) | copy-start | bytes 49156
  37.6 87.6 %copy-start.32 = (f32[4096]{0:T(1024)}, f32[4096]{0:T(1024)S(1)}, u32[]{:S(2)}) copy-start(f32[4096]{0:T(1024)S(1)} %get-tuple-element.78) | copy-start | bytes 49156
  37.6 87.6 %copy-start.34 = (f32[4096]{0:T(1024)}, f32[4096]{0:T(1024)S(1)}, u32[]{:S(2)}) copy-start(f32[4096]{0:T(1024)S(1)} %get-tuple-element.79) | copy-start | bytes 49156
  278.2 50.3 %all-to-all-start = ((bf16[4,8,4,2,64,128]{5,4,3,2,1,0:T(8,128)(2,1)}), bf16[4,8,4,2,64,128]{5,4,3,2,1,0:T(8,128)(2,1)}, u32[]{:S(2)}, u32[]{:S(2)}) async-start(bf16[4,8,4,2,64,128]{5,4,3,2,1,0:T(8,128)(2,1)} %bitcast.207), calls=%async_computation | async-start | bytes 8388608 | tf_op jit(solution)/shard_map/all_to_all | solution.py:219
  328.5 54.5 %all-to-all-start.3 = ((bf16[4,8,4,2,64,128]{5,4,3,2,1,0:T(8,128)(2,1)}), bf16[4,8,4,2,64,128]{5,4,3,2,1,0:T(8,128)(2,1)}, u32[]{:S(2)}, u32[]{:S(2)}) async-start(bf16[4,8,4,2,64,128]{5,4,3,2,1,0:T(8,128)(2,1)} %bitcast.206), calls=%async_computation.9 | async-start | bytes 8388608 | tf_op jit(solution)/shard_map/all_to_all | solution.py:219
  383.0 53.1 %all-to-all-start.2 = ((bf16[4,8,4,2,64,128]{5,4,3,2,1,0:T(8,128)(2,1)}), bf16[4,8,4,2,64,128]{5,4,3,2,1,0:T(8,128)(2,1)}, u32[]{:S(2)}, u32[]{:S(2)}) async-start(bf16[4,8,4,2,64,128]{5,4,3,2,1,0:T(8,128)(2,1)} %bitcast.205), calls=%async_computation.6 | async-start | bytes 8388608 | tf_op jit(solution)/shard_map/all_to_all | solution.py:219
  436.1 53.1 %all-to-all-start.1 = ((bf16[4,8,4,2,64,128]{5,4,3,2,1,0:T(8,128)(2,1)}), bf16[4,8,4,2,64,128]{5,4,3,2,1,0:T(8,128)(2,1)}, u32[]{:S(2)}, u32[]{:S(2)}) async-start(bf16[4,8,4,2,64,128]{5,4,3,2,1,0:T(8,128)(2,1)} %bitcast.204), calls=%async_computation.3 | async-start | bytes 8388608 | tf_op jit(solution)/shard_map/all_to_all | solution.py:219
  441.8 227.5 %reduce-scatter.11.cloned.1.call-start = ((), (), s32[]{:S(2)}) async-start(), calls=%async_computation.15 | async-start | bytes 4718592 | tf_op jit(solution)/shard_map/reduce_scatter | solution.py:231
  460.6 45.8 %copy-start.6 = (bf16[256,32,128]{2,1,0:T(8,128)(2,1)}, bf16[256,32,128]{2,1,0:T(8,128)(2,1)S(1)}, u32[]{:S(2)}) copy-start(bf16[256,32,128]{2,1,0:T(8,128)(2,1)S(1)} %fusion.192) | copy-start | bytes 6291460
  494.3 4.1 copy-start.1
  494.3 4.1 copy-start.10
  494.3 5.1 copy-start.18
  494.3 5.7 copy-start.19
  506.4 180.8 %reduce-scatter.23.cloned.1.call-start = ((), (), s32[]{:S(2)}) async-start(), calls=%async_computation.21 | async-start | bytes 4718592 | tf_op jit(solution)/shard_map/reduce_scatter | solution.py:231
  506.4 6.7 copy-start.8
  513.1 8.7 copy-start.2
  521.8 2.4 copy-start.20
  521.8 3.0 copy-start.21
  522.1 7.5 copy-start.12
  541.6 1.1 copy-start.36
  541.6 236.9 %reduce-scatter.19.cloned.1.call-start = ((), (), s32[]{:S(2)}) async-start(), calls=%async_computation.19 | async-start | bytes 4718592 | tf_op jit(solution)/shard_map/reduce_scatter | solution.py:231
  542.4 327.9 %reduce-scatter.15.cloned.1.call-start = ((), (), s32[]{:S(2)}) async-start(), calls=%async_computation.17 | async-start | bytes 4718592 | tf_op jit(solution)/shard_map/reduce_scatter | solution.py:231
  553.6 408.0 %reduce-scatter.9.cloned.1.call-start = ((), (), s32[]{:S(2)}) async-start(), calls=%async_computation.14 | async-start | bytes 4718592 | tf_op jit(solution)/shard_map/reduce_scatter | solution.py:230
  553.7 15.8 %copy-start.11 = (bf16[256,32,128]{2,1,0:T(8,128)(2,1)S(1)}, bf16[256,32,128]{2,1,0:T(8,128)(2,1)}, u32[]{:S(2)}) copy-start(bf16[256,32,128]{2,1,0:T(8,128)(2,1)} %fusion.189) | copy-start | bytes 6291460
  576.8 1.6 copy-start.13
  576.9 476.5 %reduce-scatter.13.cloned.1.call-start = ((), (), s32[]{:S(2)}) async-start(), calls=%async_computation.16 | async-start | bytes 4718592 | tf_op jit(solution)/shard_map/reduce_scatter | solution.py:230
  586.8 1.6 copy-start.9
  586.8 558.0 %reduce-scatter.17.cloned.1.call-start = ((), (), s32[]{:S(2)}) async-start(), calls=%async_computation.18 | async-start | bytes 4718592 | tf_op jit(solution)/shard_map/reduce_scatter | solution.py:230
  596.6 63.9 %copy-start.7 = (bf16[256,32,128]{2,1,0:T(8,128)(2,1)S(1)}, bf16[256,32,128]{2,1,0:T(8,128)(2,1)}, u32[]{:S(2)}) copy-start(bf16[256,32,128]{2,1,0:T(8,128)(2,1)} %copy-done.6) | copy-start | bytes 6291460
  596.6 640.1 %reduce-scatter.21.cloned.1.call-start = ((), (), s32[]{:S(2)}) async-start(), calls=%async_computation.20 | async-start | bytes 4718592 | tf_op jit(solution)/shard_map/reduce_scatter | solution.py:230
  669.2 205.6 %copy-start.3 = (f32[32,32,32]{2,1,0:T(8,128)S(1)}, f32[32,32,32]{2,1,0:T(8,128)}, u32[]{:S(2)}) copy-start(f32[32,32,32]{2,1,0:T(8,128)} %reduce-scatter.11.cloned.1.call-done) | copy-start | bytes 393220
  687.2 187.6 %copy-start.4 = (f32[32,32,32]{1,2,0:T(8,128)S(1)}, f32[32,32,32]{1,2,0:T(8,128)}, u32[]{:S(2)}) copy-start(f32[32,32,32]{1,2,0:T(8,128)} %reduce-scatter.23.cloned.1.call-done) | copy-start | bytes 393220
  778.5 96.3 %copy-start.5 = (f32[32,32,32]{1,2,0:T(8,128)S(1)}, f32[32,32,32]{1,2,0:T(8,128)}, u32[]{:S(2)}) copy-start(f32[32,32,32]{1,2,0:T(8,128)} %reduce-scatter.19.cloned.1.call-done) | copy-start | bytes 393220
  877.2 176.2 %copy-start.25 = (f32[32,32,32]{1,2,0:T(8,128)S(1)}, f32[32,32,32]{1,2,0:T(8,128)}, u32[]{:S(2)}) copy-start(f32[32,32,32]{1,2,0:T(8,128)} %get-tuple-element.20) | copy-start | bytes 393220
  877.2 176.2 %copy-start.26 = (f32[32,32,32]{1,2,0:T(8,128)S(1)}, f32[32,32,32]{1,2,0:T(8,128)}, u32[]{:S(2)}) copy-start(f32[32,32,32]{1,2,0:T(8,128)} %get-tuple-element.21) | copy-start | bytes 393220
  877.2 176.2 %copy-start.27 = (f32[32,32,32]{1,2,0:T(8,128)S(1)}, f32[32,32,32]{1,2,0:T(8,128)}, u32[]{:S(2)}) copy-start(f32[32,32,32]{1,2,0:T(8,128)} %get-tuple-element.65) | copy-start | bytes 393220
  961.6 4.9 copy-start.17
  966.8 178.0 %copy-start.24 = (f32[32,32,32]{2,1,0:T(8,128)S(1)}, f32[32,32,32]{2,1,0:T(8,128)}, u32[]{:S(2)}) copy-start(f32[32,32,32]{2,1,0:T(8,128)} %get-tuple-element.109) | copy-start | bytes 393220
  1053.4 3.9 copy-start.15
  1144.8 4.6 copy-start.14
  1236.7 4.9 copy-start.16
  1304.5 19.0 %all-to-all-start.5 = ((bf16[2,8,8,4,1024]{4,2,1,0,3:T(8,128)(2,1)}), bf16[2,8,8,4,1024]{4,2,1,0,3:T(8,128)(2,1)S(1)}, u32[]{:S(2)}, u32[]{:S(2)}) async-start(bf16[2,8,8,4,1024]{4,2,1,0,3:T(8,128)(2,1)} %copy.238), calls=%async_computation.13 | async-start | bytes 2097152 | tf_op jit(solution)/shard_map/all_to_all | solution.py:241
  1342.0 6.3 copy-start.23
  1368.6 8.9 collective-permute-start.1
  (5 other events, 4.4 us)
Sparse Core Ops, SparseCore 0:
  506.5 88.5 reduce-scatter.10
  599.2 87.9 reduce-scatter.22
  690.8 87.6 reduce-scatter.18
  782.4 87.8 reduce-scatter.14
  873.8 87.7 reduce-scatter.8
  965.5 87.8 reduce-scatter.12
  1057.0 87.7 reduce-scatter.16
  1148.9 87.8 reduce-scatter.20

commit v2 on v1

--- a/solution.py
+++ b/solution.py
@@ -202,6 +202,7 @@
     steps = jnp.arange(RADIX, dtype=jnp.int32).astype(jnp.float32)
     high_cos, high_sin = rotation(math.pi * RADIX / length * steps, delay)
 
+    samples, loading = lax.optimization_barrier((samples, loading))
     turned = first_stage(halo_filter(samples))
     turned = turned.reshape(
         block_dev, section_count, rows_dev, 2 * RADIX, inputs_dev
@@ -227,8 +228,13 @@
         ).astype(jnp.bfloat16)
         steer = steer.reshape(rows_piece * RADIX, beam_total, 2 * inputs_dev)
         projected, packed = local_products(spectra, steer)
-        projected = lax.psum_scatter(projected, "gx", scatter_dimension=0, tiled=True)
-        packed = lax.psum_scatter(packed, "gx", scatter_dimension=0, tiled=True)
+        chans = projected.shape[0]
+        projected = lax.psum_scatter(
+            projected.reshape(chans, -1), "gx", scatter_dimension=0, tiled=True
+        ).reshape(-1, beam_total, 2 * snapshots)
+        packed = lax.psum_scatter(
+            packed.reshape(chans, -1), "gx", scatter_dimension=0, tiled=True
+        ).reshape(-1, snapshots, snapshots)
         formed.append(solve(projected, packed, loading[piece], inputs_all))
 
     beam_spec = jnp.stack(formed, axis=1)

time: 1390 us -> 1300 us (0.935)
  waiting for transfers between devices: 770 us -> 622 us
  local copies, waits for them, and re-layouts: 262 us -> 326 us
    reduce_scatter x8 -> x0, waiting for transfers between devices: 541 us -> none  [the longest x4 344 us: body(): lax.psum_scatter(projected, 'gx', scatter_dimension=0, tiled=True)]
    unnamed x8 -> x16, waiting for transfers between devices: 0.8 us -> 394 us
    optimization_barrier x0 -> x1, local copies, waits for them, and re-layouts: none -> 22.4 us  [body(): samples, loading = lax.optimization_barrier((samples, loading))]
    convert_element_type x0 -> x4, local copies, waits for them, and re-layouts: none -> 19.7 us  [local_products(): return (projected.astype(jnp.bfloat16), packed)]
    select_n x0 -> x4, local copies, waits for them, and re-layouts: none -> 14.1 us  [local_products(): packed = jnp.where(row <= col, gram[..., :snapshots], gram[..., snapshots:])]
    unnamed x81 -> x78, local copies, waits for them, and re-layouts: 59.6 us -> 59.9 us
  transfers between devices with their start and end apart: 15 -> 15, of which waited for: 14 -> 14; matrix products, arithmetic and copies ran while one was open for 12% -> 15% of each run, Pallas kernels for 0% -> 0%
where the time goes in v2:
time: 1300 us
  waiting for transfers between devices  622 us (48%)
  local copies, waits for them, and re-layouts  326 us (25%)
  other arithmetic  109 us (8%)
  matrix products  90.2 us (7%)
  blocking collectives  89.8 us (7%)
  starting transfers between devices  43.2 us (3%)
  between operations  14.8 us (1%)
    unnamed x16, waiting for transfers between devices  394 us
    all_to_all x4, waiting for transfers between devices, body(): lax.all_to_all(spectra, 'section', split_axis=0, concat_axis=0, tiled=True)  141 us
    ppermute x2, waiting for transfers between devices, from_behind(): lax.ppermute(value, axis, [(source, source + steps) for source in range(i...  73.1 us
    all_gather x1, blocking collectives, body(): loading = lax.all_gather(loading, ('section', 'gx'), tiled=True)  61.3 us
    unnamed x78, local copies, waits for them, and re-layouts  59.9 us
    dot_general x4, matrix products, local_products(): jnp.einsum('fbm,fkm->fbk', steer, blocked, preferred_element_type=jnp.flo...  33 us
    transpose x1, local copies, waits for them, and re-layouts, first_stage(): jnp.einsum('fi,kiz->kfz', matrix, by_input, preferred_element_type=jnp.fl...  31.1 us
    all_to_all x1, blocking collectives, body(): lax.all_to_all(packed_back, 'gx', split_axis=1, concat_axis=1, tiled=True)  28.5 us
  transfers between devices with their start and end apart: 15, of which 14 were waited for; matrix products, arithmetic and copies ran while one was open for 15% of the time, Pallas kernels for 0%

profile of v2, /device:TPU:1, one launch (start us, length us, event | category | flops | bytes accessed | tf_op | source)
XLA Modules:
  0.0 1295.3 jit_solution(3074006073236624397)
XLA Ops:
  7.2 61.3 %all-gather = f32[32,1,128]{2,1,0:T(1,128)S(1)} all-gather(f32[1,1,128]{2,1,0:T(1,128)S(1)} %exponential_bitcast_fusion), channel_id=1, replica_groups=mesh['section'=4,'gx'=8] {'section','gx'}, dimensions={0}, use_global_device_ids=true | all-gather | bytes 16896 | tf_op jit(solution)/shard_map/all_gather | solution.py:188
  70.6 22.4 %copy.140 = bf16[2,128,8,4096]{1,3,2,0:T(8,128)(2,1)} copy(bf16[2,128,8,4096]{3,2,1,0:T(8,128)(2,1)} %param.5) | data formatting | bytes 33554432 | tf_op jit(solution)/shard_map/optimization_barrier | solution.py:205
  96.3 10.0 collective-permute-start
  107.2 67.0 %collective-permute-done = bf16[2,128,3,4096]{1,3,2,0:T(8,128)(2,1)S(1)} collective-permute-done((bf16[2,128,3,4096]{1,3,2,0:T(8,128)(2,1)S(1)}, bf16[2,128,3,4096]{1,3,2,0:T(8,128)(2,1)S(1)}, u32[]{:S(2)}, u32[]{:S(2)}) %collective-permute-start) | collective-permute-done | bytes 6291488 | tf_op jit(solution)/shard_map/ppermute | solution.py:17
  174.2 20.9 %add_convert_fusion = bf16[2,128,8,4096]{1,3,2,0:T(8,128)(2,1)S(1)} fusion(bf16[2,128,8,4096]{1,3,2,0:T(8,128)(2,1)} %copy.140, bf16[2,128,3,4096]{1,3,2,0:T(8,128)(2,1)S(1)} %collective-permute-done, f32[4096]{0:T(1024)S(1)} %get-tuple-element.75, f32[4096]{0:T(1024)S(1)} %get-tuple-element.73, f32[4096]{0:T(1024)S(1)} %get-tuple-element.74, ...), kind=kLoop, calls=%fused_computation | loop fusion | flops 125829120 | bytes 39911424 | tf_op jit(solution)/shard_map/convert_element_type | solution.py:65
  195.2 6.8 copy.143
  201.9 25.3 %reshape.1183 = bf16[8,128,8192]{2,1,0:T(8,128)(2,1)} reshape(bf16[8,2,64,64,128]{4,3,2,1,0:T(8,128)(2,1)} %copy.143) | data formatting | bytes 33554432 | tf_op jit(solution)/shard_map/reshape | solution.py:73
  227.2 16.6 %convolution_bitcast_fusion = f32[8,128,8192]{1,2,0:T(8,128)} fusion(bf16[8,128,8192]{2,1,0:T(8,128)(2,1)} %reshape.1183, bf16[64,64]{1,0:T(8,128)(2,1)S(1)} %get-tuple-element.128, bf16[64,64]{1,0:T(8,128)(2,1)S(1)} %get-tuple-element.127, bf16[64,64]{1,0:T(8,128)(2,1)S(1)} %fusion.157), kind=kOutput, calls=%fused_computation.11 | convolution fusion | flops 2147614720 | bytes 50356224 | tf_op jit(solution)/shard_map/fi,kiz->kfz/dot_general | solution.py:74
  243.8 31.1 %copy.145 = f32[8,128,8192]{2,1,0:T(8,128)} copy(f32[8,128,8192]{1,2,0:T(8,128)} %convolution_bitcast_fusion) | data formatting | bytes 67108864 | tf_op jit(solution)/shard_map/fi,kiz->kfz/transpose | solution.py:74
  274.9 27.6 %copy.240 = f32[128,8,64,128]{3,2,1,0:T(8,128)} copy(f32[128,8,64,128]{3,1,2,0:T(8,128)} %bitcast.218) | data formatting | bytes 67108864
  302.5 17.0 %fusion.197 = (f32[8,1,64,64,128]{4,3,2,1,0:T(8,128)S(1)}, f32[8,1,64,64,128]{4,3,2,1,0:T(8,128)}) fusion(f32[8,2,64,64,128]{4,3,2,1,0:T(8,128)} %bitcast.217), kind=kLoop, calls=%fused_computation.357 | loop fusion | bytes 67108864 | tf_op jit(solution)/shard_map/slice | solution.py:77
  319.5 14.1 %subtract_convert_fusion = (bf16[8,4,16,64,128]{4,3,2,1,0:T(8,128)(2,1)}, bf16[8,4,16,64,128]{4,3,2,1,0:T(8,128)(2,1)}) fusion(f32[8,4,16,64,128]{4,3,2,1,0:T(8,128)S(1)} %bitcast.220, f32[8,4,16,64,128]{4,3,2,1,0:T(8,128)} %bitcast.221, f32[4,16,64]{2,1,0:T(8,128)S(1)} %get-tuple-element.118, f32[4,16,64]{2,1,0:T(8,128)S(1)} %get-tuple-element.117), kind=kLoop, calls=%fused_computation.16 | loop fusion | flops 33554432 | bytes 50364416 | tf_op jit(solution)/shard_map/convert_element_type | solution.py:77
  333.5 10.2 fusion.19
  348.0 5.4 all-to-all-start.1
  359.8 38.8 %all-to-all-done.1 = bf16[4,8,4,2,64,128]{5,4,3,2,1,0:T(8,128)(2,1)} async-done(((bf16[4,8,4,2,64,128]{5,4,3,2,1,0:T(8,128)(2,1)}), bf16[4,8,4,2,64,128]{5,4,3,2,1,0:T(8,128)(2,1)}, u32[]{:S(2)}, u32[]{:S(2)}) %all-to-all-start.1) | async-done | bytes 4194336 | tf_op jit(solution)/shard_map/all_to_all | solution.py:220
  398.6 7.1 all-to-all-start
  412.2 40.9 %all-to-all-done = bf16[4,8,4,2,64,128]{5,4,3,2,1,0:T(8,128)(2,1)} async-done(((bf16[4,8,4,2,64,128]{5,4,3,2,1,0:T(8,128)(2,1)}), bf16[4,8,4,2,64,128]{5,4,3,2,1,0:T(8,128)(2,1)}, u32[]{:S(2)}, u32[]{:S(2)}) %all-to-all-start) | async-done | bytes 4194336 | tf_op jit(solution)/shard_map/all_to_all | solution.py:220
  453.2 5.7 all-to-all-start.2
  465.3 41.0 %all-to-all-done.2 = bf16[4,8,4,2,64,128]{5,4,3,2,1,0:T(8,128)(2,1)} async-done(((bf16[4,8,4,2,64,128]{5,4,3,2,1,0:T(8,128)(2,1)}), bf16[4,8,4,2,64,128]{5,4,3,2,1,0:T(8,128)(2,1)}, u32[]{:S(2)}, u32[]{:S(2)}) %all-to-all-start.2) | async-done | bytes 4194336 | tf_op jit(solution)/shard_map/all_to_all | solution.py:220
  506.3 5.7 all-to-all-start.3
  538.8 20.6 %all-to-all-done.3 = bf16[4,8,4,2,64,128]{5,4,3,2,1,0:T(8,128)(2,1)} async-done(((bf16[4,8,4,2,64,128]{5,4,3,2,1,0:T(8,128)(2,1)}), bf16[4,8,4,2,64,128]{5,4,3,2,1,0:T(8,128)(2,1)}, u32[]{:S(2)}, u32[]{:S(2)}) %all-to-all-start.3) | async-done | bytes 4194336 | tf_op jit(solution)/shard_map/all_to_all | solution.py:220
  559.4 5.3 copy.181
  587.3 14.9 %slice_select_fusion.3 = (f32[256,32,32]{2,1,0:T(8,128)}, f32[256,32,32]{2,1,0:T(8,128)}, f32[256,32,32]{2,1,0:T(8,128)}, f32[256,32,32]{2,1,0:T(8,128)}) fusion(f32[256,32,64]{2,1,0:T(8,128)} %fusion.24, pred[32,32]{1,0:T(8,128)(4,1)S(1)} %iota_compare_fusion.2, f32[256,32,64]{2,1,0:T(8,128)S(1)} %fusion.28, f32[256,32,64]{2,1,0:T(8,128)} %fusion.32, ...), kind=kLoop, calls=%fused_computation.61 | loop fusion | flops 1048576 | bytes 12583936 | tf_op jit(solution)/shard_map/jit(_where)/select_n | solution.py:103
  620.1 8.7 multiply_cosine_fusion
  633.7 14.6 %subtract_convert_fusion.4 = (bf16[4,64,64,128]{3,2,1,0:T(8,128)(2,1)}, bf16[4,64,64,128]{3,2,1,0:T(8,128)(2,1)}, bf16[4,64,64,128]{3,2,1,0:T(8,128)(2,1)}, bf16...) fusion(f32[64,64,128]{2,1,0:T(8,128)} %get-tuple-element.85, ...), kind=kLoop, calls=%fused_computation.48 | loop fusion | flops 67108864 | bytes 38797312 | tf_op jit(solution)/shard_map/convert.41
  648.3 6.0 fusion.40
  654.3 4.9 copy.182
  662.2 8.9 fusion.43
  671.2 4.9 copy.171
  679.2 9.0 fusion.46
  688.2 5.0 copy.160
  696.3 9.2 fusion.49
  705.5 4.9 copy.148
  716.0 15.5 %reduce-scatter.31.cloned.1.call-done = f32[32,1024]{1,0:T(8,128)} async-done(((f32[256,1024]{1,0:T(8,128)}), f32[32,1024]{1,0:T(8,128)}) %reduce-scatter.31.cloned.1.call-update) | async-done | bytes 131088
  733.6 63.7 %reduce-scatter.35.cloned.1.call-done = f32[32,1024]{1,0:T(8,128)} async-done(((f32[256,1024]{1,0:T(8,128)}), f32[32,1024]{1,0:T(8,128)}) %reduce-scatter.35.cloned.1.call-update) | async-done | bytes 131088
  800.2 63.6 %reduce-scatter.39.cloned.1.call-done = f32[32,1024]{1,0:T(8,128)} async-done(((f32[256,1024]{1,0:T(8,128)}), f32[32,1024]{1,0:T(8,128)}) %reduce-scatter.39.cloned.1.call-update) | async-done | bytes 131088
  871.6 62.1 %reduce-scatter.37.cloned.1.call-done = bf16[32,4096]{1,0:T(8,128)(2,1)} async-done(((bf16[256,4096]{1,0:T(8,128)(2,1)}), bf16[32,4096]{1,0:T(8,128)(2,1)}) %reduce-scatter.37.cloned.1.call-update) | async-done | bytes 262160
  940.2 63.7 %reduce-scatter.33.cloned.1.call-done = bf16[32,4096]{1,0:T(8,128)(2,1)} async-done(((bf16[256,4096]{1,0:T(8,128)(2,1)}), bf16[32,4096]{1,0:T(8,128)(2,1)}) %reduce-scatter.33.cloned.1.call-update) | async-done | bytes 262160
  1011.5 62.9 %reduce-scatter.29.cloned.1.call-done = bf16[32,4096]{1,0:T(8,128)(2,1)} async-done(((bf16[256,4096]{1,0:T(8,128)(2,1)}), bf16[32,4096]{1,0:T(8,128)(2,1)}) %reduce-scatter.29.cloned.1.call-update) | async-done | bytes 262160
  1082.1 62.8 %reduce-scatter.25.cloned.1.call-done = bf16[32,4096]{1,0:T(8,128)(2,1)} async-done(((bf16[256,4096]{1,0:T(8,128)(2,1)}), bf16[32,4096]{1,0:T(8,128)(2,1)}) %reduce-scatter.25.cloned.1.call-update) | async-done | bytes 262160
  1167.8 7.8 copy.221
  1175.5 8.5 reshape.1184
  1184.1 28.5 %all_to_all.30 = bf16[2,8,8,4,1024]{4,2,3,0,1:T(8,128)(2,1)S(1)} all-to-all(bf16[2,8,8,4,1024]{4,2,3,0,1:T(8,128)(2,1)S(1)} %reshape.1184), channel_id=1, replica_groups=mesh['section'=4,'gx'=8] {'gx'}, dimensions={1} | all-to-all | bytes 2097152 | tf_op jit(solution)/shard_map/all_to_all | solution.py:248
  1213.7 5.9 all-to-all-start.5
  1220.0 13.1 %all-to-all-done.5 = bf16[2,8,8,4,1024]{4,2,1,0,3:T(8,128)(2,1)S(1)} async-done(((bf16[2,8,8,4,1024]{4,2,1,0,3:T(8,128)(2,1)}), bf16[2,8,8,4,1024]{4,2,1,0,3:T(8,128)(2,1)S(1)}, u32[]{:S(2)}, u32[]{:S(2)}) %all-to-all-start.5) | async-done | bytes 1048608 | tf_op jit(solution)/shard_map/all_to_all | solution.py:247
  1237.5 9.1 copy.247
  1246.5 5.0 reshape_reshape.3
  1280.9 6.1 collective-permute-done.1
  (220 shorter events, 210.4 us)
Async XLA Ops:
  6.5 610.6 %copy-start = (f32[2,1024]{1,0:T(2,128)S(1)}, f32[2,1024]{1,0:T(2,128)}, u32[]{:S(2)}) copy-start(f32[2,1024]{1,0:T(2,128)} %param.6) | copy-start | bytes 24580
  96.3 77.9 %collective-permute-start = (bf16[2,128,3,4096]{1,3,2,0:T(8,128)(2,1)S(1)}, bf16[2,128,3,4096]{1,3,2,0:T(8,128)(2,1)S(1)}, u32[]{:S(2)}, u32[]{:S(2)}) collective-permute-start(bf16[2,128,3,4096]{1,3,2,0:T(8,128)(2,1)S(1)} %slice.274), channel_id=1, source_target_pairs={{0,8},{8,16},{16,24},{1,9},{9,17},{17,25},{2,10},{10,18},{18,26},{... | collective-permute-start | bytes 18874376 | tf_op jit(solution)/shard_map/ppermute | solution.py:17
  106.6 352.3 %copy-start.17 = (bf16[64,64]{1,0:T(8,128)(2,1)}, bf16[64,64]{1,0:T(8,128)(2,1)S(1)}, u32[]{:S(2)}) copy-start(bf16[64,64]{1,0:T(8,128)(2,1)S(1)} %get-tuple-element.128) | copy-start | bytes 24580
  107.1 88.0 %copy-start.20 = (f32[4096]{0:T(1024)}, f32[4096]{0:T(1024)S(1)}, u32[]{:S(2)}) copy-start(f32[4096]{0:T(1024)S(1)} %get-tuple-element.72) | copy-start | bytes 49156
  107.2 88.0 %copy-start.22 = (f32[4096]{0:T(1024)}, f32[4096]{0:T(1024)S(1)}, u32[]{:S(2)}) copy-start(f32[4096]{0:T(1024)S(1)} %get-tuple-element.73) | copy-start | bytes 49156
  107.2 88.0 %copy-start.24 = (f32[4096]{0:T(1024)}, f32[4096]{0:T(1024)S(1)}, u32[]{:S(2)}) copy-start(f32[4096]{0:T(1024)S(1)} %get-tuple-element.74) | copy-start | bytes 49156
  107.2 88.0 %copy-start.26 = (f32[4096]{0:T(1024)}, f32[4096]{0:T(1024)S(1)}, u32[]{:S(2)}) copy-start(f32[4096]{0:T(1024)S(1)} %get-tuple-element.75) | copy-start | bytes 49156
  348.0 50.6 %all-to-all-start.1 = ((bf16[4,8,4,2,64,128]{5,4,3,2,1,0:T(8,128)(2,1)}), bf16[4,8,4,2,64,128]{5,4,3,2,1,0:T(8,128)(2,1)}, u32[]{:S(2)}, u32[]{:S(2)}) async-start(bf16[4,8,4,2,64,128]{5,4,3,2,1,0:T(8,128)(2,1)} %bitcast.235), calls=%async_computation.1 | async-start | bytes 8388608 | tf_op jit(solution)/shard_map/all_to_all | solution.py:220
  398.6 54.5 %all-to-all-start = ((bf16[4,8,4,2,64,128]{5,4,3,2,1,0:T(8,128)(2,1)}), bf16[4,8,4,2,64,128]{5,4,3,2,1,0:T(8,128)(2,1)}, u32[]{:S(2)}, u32[]{:S(2)}) async-start(bf16[4,8,4,2,64,128]{5,4,3,2,1,0:T(8,128)(2,1)} %bitcast.234), calls=%async_computation | async-start | bytes 8388608 | tf_op jit(solution)/shard_map/all_to_all | solution.py:220
  453.2 53.1 %all-to-all-start.2 = ((bf16[4,8,4,2,64,128]{5,4,3,2,1,0:T(8,128)(2,1)}), bf16[4,8,4,2,64,128]{5,4,3,2,1,0:T(8,128)(2,1)}, u32[]{:S(2)}, u32[]{:S(2)}) async-start(bf16[4,8,4,2,64,128]{5,4,3,2,1,0:T(8,128)(2,1)} %bitcast.233), calls=%async_computation.2 | async-start | bytes 8388608 | tf_op jit(solution)/shard_map/all_to_all | solution.py:220
  506.3 53.1 %all-to-all-start.3 = ((bf16[4,8,4,2,64,128]{5,4,3,2,1,0:T(8,128)(2,1)}), bf16[4,8,4,2,64,128]{5,4,3,2,1,0:T(8,128)(2,1)}, u32[]{:S(2)}, u32[]{:S(2)}) async-start(bf16[4,8,4,2,64,128]{5,4,3,2,1,0:T(8,128)(2,1)} %bitcast.232), calls=%async_computation.3 | async-start | bytes 8388608 | tf_op jit(solution)/shard_map/all_to_all | solution.py:220
  512.0 201.8 %reduce-scatter.27.cloned.1.call-start = ((), (), s32[]{:S(2)}) async-start(), calls=%async_computation.15 | async-start | bytes 1179648
  527.2 46.1 %copy-start.4 = (bf16[256,32,128]{2,1,0:T(8,128)(2,1)}, bf16[256,32,128]{2,1,0:T(8,128)(2,1)S(1)}, u32[]{:S(2)}) copy-start(bf16[256,32,128]{2,1,0:T(8,128)(2,1)S(1)} %fusion.185) | copy-start | bytes 6291460
  565.0 13.0 copy-start.7
  565.0 3.2 copy-start.5
  565.0 4.4 copy-start.11
  565.0 5.0 copy-start.12
  565.8 12.2 copy-start.15
  565.8 12.2 copy-start.16
  570.1 3.2 copy-start.9
  570.1 3.2 copy-start.10
  577.9 4.7 copy-start.6
  578.0 4.7 copy-start.13
  578.0 4.7 copy-start.14
  607.0 124.4 %reduce-scatter.31.cloned.1.call-start = ((), (), s32[]{:S(2)}) async-start(), calls=%async_computation.17 | async-start | bytes 1179648
  612.0 185.3 %reduce-scatter.35.cloned.1.call-start = ((), (), s32[]{:S(2)}) async-start(), calls=%async_computation.19 | async-start | bytes 1179648
  612.0 5.1 copy-start.29
  616.9 246.9 %reduce-scatter.39.cloned.1.call-start = ((), (), s32[]{:S(2)}) async-start(), calls=%async_computation.21 | async-start | bytes 1179648
  633.7 300.0 %reduce-scatter.37.cloned.1.call-start = ((), (), s32[]{:S(2)}) async-start(), calls=%async_computation.20 | async-start | bytes 2359296
  633.7 14.6 %copy-start.8 = (bf16[256,32,128]{2,1,0:T(8,128)(2,1)S(1)}, bf16[256,32,128]{2,1,0:T(8,128)(2,1)}, u32[]{:S(2)}) copy-start(bf16[256,32,128]{2,1,0:T(8,128)(2,1)} %copy-done.7) | copy-start | bytes 6291460
  662.2 341.8 %reduce-scatter.33.cloned.1.call-start = ((), (), s32[]{:S(2)}) async-start(), calls=%async_computation.18 | async-start | bytes 2359296
  679.1 395.3 %reduce-scatter.29.cloned.1.call-start = ((), (), s32[]{:S(2)}) async-start(), calls=%async_computation.16 | async-start | bytes 2359296
  693.1 3.1 copy-start.28
  696.1 448.8 %reduce-scatter.25.cloned.1.call-start = ((), (), s32[]{:S(2)}) async-start(), calls=%async_computation.14 | async-start | bytes 2359296
  1010.5 1.1 copy-start.2
  1077.7 4.3 copy-start.3
  1150.6 4.1 copy-start.19
  1213.7 19.5 %all-to-all-start.5 = ((bf16[2,8,8,4,1024]{4,2,1,0,3:T(8,128)(2,1)}), bf16[2,8,8,4,1024]{4,2,1,0,3:T(8,128)(2,1)S(1)}, u32[]{:S(2)}, u32[]{:S(2)}) async-start(bf16[2,8,8,4,1024]{4,2,1,0,3:T(8,128)(2,1)} %copy.193), calls=%async_computation.5 | async-start | bytes 2097152 | tf_op jit(solution)/shard_map/all_to_all | solution.py:247
  1251.6 6.3 copy-start.18
  1275.1 0.9 copy-start.21
  1275.2 0.9 copy-start.23
  1275.2 0.9 copy-start.25
  1275.2 0.9 copy-start.27
  1276.1 12.1 copy-start.1
  1278.1 8.9 collective-permute-start.1
Sparse Core Ops, SparseCore 0:
  607.2 58.1 reduce-scatter.26
  669.1 62.2 reduce-scatter.30
  734.9 62.3 reduce-scatter.34
  800.9 62.8 reduce-scatter.38
  867.2 66.4 reduce-scatter.36
  937.1 66.8 reduce-scatter.32
  1007.5 66.8 reduce-scatter.28
  1078.0 66.8 reduce-scatter.24

commit v3 on v1

--- a/solution.py
+++ b/solution.py
@@ -3,12 +3,14 @@
 import jax
 import jax.numpy as jnp
 from jax import lax
+from jax.experimental import pallas as pl
+from jax.experimental.pallas import tpu as pltpu
 from jax.sharding import PartitionSpec as P
 
 RADIX = 64
 TAPS = 4
 ITERS = 2
-PIECES = 4
+PIECES = 2
 
 
 def from_behind(value, axis, steps):
@@ -51,38 +53,125 @@
     return jnp.concatenate([top, bottom], axis=0), twist_cos, direction_sign * twist_sin
 
 
-def halo_filter(samples):
+def with_halo(samples):
     block_dev = samples.shape[2]
-    history = TAPS - 1
-    shaping = prototype(TAPS, samples.shape[3])
-    earlier = from_behind(samples[:, :, block_dev - history :, :], "section", 1)
-    extended = jnp.concatenate([earlier, samples], axis=2)
-    filtered = shaping[0] * extended[:, :, history : history + block_dev, :].astype(jnp.float32)
-    for tap_index in range(1, TAPS):
-        filtered = filtered + shaping[tap_index] * extended[
-            :, :, history - tap_index : history - tap_index + block_dev, :
-        ].astype(jnp.float32)
-    return filtered.astype(jnp.bfloat16)
-
-
-def first_stage(filtered):
-    _, inputs_dev, block_dev, _ = filtered.shape
+    turned = jnp.transpose(samples, (2, 0, 3, 1))
+    earlier = from_behind(turned[block_dev - (TAPS - 1) :], "section", 1)
+    return jnp.concatenate([earlier, turned], axis=0)
+
+
+def split_rows(matrix, parts):
+    rows = matrix.reshape(2, parts, RADIX // parts, matrix.shape[1])
+    return jnp.transpose(rows, (1, 0, 2, 3)).reshape(matrix.shape)
+
+
+def analysis_kernel(parts, x3, x2, x1, x0, proto, first, second, tcos, tsin, *rest):
+    outs, (filt, turn) = rest[:-2], rest[-2:]
+    length = x0.shape[2]
+    chunk = 128
+
+    def filter_step(step, carry):
+        rows = pl.ds(pl.multiple_of(step * chunk, chunk), chunk)
+        for c in range(2):
+            total = proto[0, rows, :] * x0[0, c, rows, :].astype(jnp.float32)
+            for tap, ref in ((1, x1), (2, x2), (3, x3)):
+                total = total + proto[tap, rows, :] * ref[0, c, rows, :].astype(jnp.float32)
+            place = pl.ds(pl.multiple_of(c * length + step * chunk, chunk), chunk)
+            filt[place, :] = total
+        return carry
+
+    lax.fori_loop(0, length // chunk, filter_step, 0)
+
+    def first_step(l, carry):
+        z = jnp.concatenate(
+            [filt[pl.ds(l, RADIX, stride=RADIX), :], filt[pl.ds(length + l, RADIX, stride=RADIX), :]],
+            axis=0,
+        ).astype(jnp.bfloat16)
+        mid = jnp.dot(first[...], z, preferred_element_type=jnp.float32)
+        real, imag = mid[:RADIX], mid[RADIX:]
+        cos_col, sin_col = tcos[l], tsin[l]
+        turn[pl.ds(l, RADIX, stride=RADIX), :] = real * cos_col - imag * sin_col
+        turn[pl.ds(length + l, RADIX, stride=RADIX), :] = imag * cos_col + real * sin_col
+        return carry
+
+    lax.fori_loop(0, RADIX, first_step, 0, unroll=8)
+
+    rows_piece = RADIX // len(outs)
+    wide = 2 * RADIX // parts
+    for piece, out in enumerate(outs):
+
+        def second_step(a, carry, piece=piece, out=out):
+            base = pl.multiple_of((piece * rows_piece + a) * RADIX, RADIX)
+            t = jnp.concatenate(
+                [turn[pl.ds(base, RADIX), :], turn[pl.ds(base + length, RADIX), :]], axis=0
+            ).astype(jnp.bfloat16)
+            spec = jnp.dot(second[...], t, preferred_element_type=jnp.float32)
+            spec = (spec * (1.0 / RADIX)).astype(jnp.bfloat16)
+            for part in range(parts):
+                out[part, 0, a] = spec[part * wide : (part + 1) * wide]
+            return carry
+
+        lax.fori_loop(0, rows_piece, second_step, 0, unroll=8)
+
+
+def analysis(samples, parts):
+    extended = with_halo(samples)
+    blocks = extended.shape[0] - (TAPS - 1)
+    _, _, length, inputs_dev = extended.shape
     matrix, twist_cos, twist_sin = stacked_tables(-1.0)
-    by_input = jnp.transpose(
-        filtered.reshape(2, inputs_dev, block_dev, RADIX, RADIX), (2, 0, 3, 4, 1)
-    ).reshape(block_dev, 2 * RADIX, RADIX * inputs_dev)
-    mid = jnp.einsum("fi,kiz->kfz", matrix, by_input, preferred_element_type=jnp.float32)
-    mid = mid.reshape(block_dev, 2, RADIX, RADIX, inputs_dev)
+    second = split_rows(matrix, parts)
+    shaping = prototype(TAPS, length)
+    rows_piece = RADIX // PIECES
+    wide = 2 * RADIX // parts
+    if inputs_dev % 128 == 0:
+        proto = jnp.broadcast_to(shaping[..., None], (TAPS, length, inputs_dev))
+        table = (RADIX, RADIX, inputs_dev)
+        tcos = jnp.broadcast_to(jnp.transpose(twist_cos)[..., None], table)
+        tsin = jnp.broadcast_to(jnp.transpose(twist_sin)[..., None], table)
+
+        def whole(shape):
+            return pl.BlockSpec(shape, lambda k: (0,) * len(shape), pipeline_mode=pl.Buffered(1))
+
+        def shifted(shift):
+            return pl.BlockSpec((1, 2, length, inputs_dev), lambda k: (k + shift, 0, 0, 0))
+
+        return pl.pallas_call(
+            lambda *refs: analysis_kernel(parts, *refs),
+            grid=(blocks,),
+            in_specs=[shifted(p) for p in range(TAPS)]
+            + [whole(v.shape) for v in (proto, matrix, second, tcos, tsin)],
+            out_specs=[
+                pl.BlockSpec((parts, 1, rows_piece, wide, inputs_dev), lambda k: (0, k, 0, 0, 0))
+            ]
+            * PIECES,
+            out_shape=[
+                jax.ShapeDtypeStruct((parts, blocks, rows_piece, wide, inputs_dev), jnp.bfloat16)
+            ]
+            * PIECES,
+            scratch_shapes=[pltpu.VMEM((2 * length, inputs_dev), jnp.float32)] * 2,
+            compiler_params=pltpu.CompilerParams(vmem_limit_bytes=56 * 1024 * 1024),
+            cost_estimate=pl.CostEstimate(
+                flops=blocks * inputs_dev * length * 1024,
+                bytes_accessed=blocks * inputs_dev * length * 20,
+                transcendentals=0,
+            ),
+        )(extended, extended, extended, extended, proto, matrix, second, tcos, tsin)
+    filtered = sum(
+        shaping[p][:, None] * extended[TAPS - 1 - p : TAPS - 1 - p + blocks].astype(jnp.float32)
+        for p in range(TAPS)
+    ).astype(jnp.bfloat16)
+    z = filtered.reshape(blocks, 2 * RADIX, RADIX * inputs_dev)
+    mid = jnp.einsum("fi,kiz->kfz", matrix, z, preferred_element_type=jnp.float32)
+    mid = mid.reshape(blocks, 2, RADIX, RADIX, inputs_dev)
     cos_col, sin_col = twist_cos[..., None], twist_sin[..., None]
     real = (mid[:, 0] * cos_col - mid[:, 1] * sin_col).astype(jnp.bfloat16)
     imag = (mid[:, 1] * cos_col + mid[:, 0] * sin_col).astype(jnp.bfloat16)
-    return jnp.concatenate([real, imag], axis=2)
-
-
-def second_stage(turned):
-    matrix, _, _ = stacked_tables(-1.0)
-    out = jnp.einsum("gl,kalm->kagm", matrix, turned, preferred_element_type=jnp.float32)
-    return (out * (1.0 / RADIX)).astype(jnp.bfloat16)
+    turned = jnp.concatenate([real, imag], axis=2)
+    out = jnp.einsum("gl,kalm->kagm", second, turned, preferred_element_type=jnp.float32)
+    out = (out * (1.0 / RADIX)).astype(jnp.bfloat16)
+    out = out.reshape(blocks, PIECES, rows_piece, parts, wide, inputs_dev)
+    out = jnp.transpose(out, (1, 3, 0, 2, 4, 5))
+    return [out[piece] for piece in range(PIECES)]
 
 
 def rotation(scale, delay):
@@ -148,11 +237,11 @@
 
 def synthesis_transform(values):
     matrix, twist_cos, twist_sin = stacked_tables(1.0)
-    _, beams, blocks, _, _ = values.shape
+    _, beams, blocks, pieces, _, rows_piece = values.shape
     rows = beams * blocks
-    z = jnp.transpose(values.reshape(2, rows, RADIX, RADIX), (0, 3, 1, 2)).reshape(
-        2 * RADIX, rows * RADIX
-    )
+    z = jnp.transpose(
+        values.reshape(2, rows, pieces, RADIX, rows_piece), (0, 3, 1, 2, 4)
+    ).reshape(2 * RADIX, rows * RADIX)
     mid = jnp.einsum("fi,iz->fz", matrix, z, preferred_element_type=jnp.float32)
     mid = mid.reshape(2, RADIX, rows, RADIX)
     cos_col, sin_col = twist_cos[:, None, :], twist_sin[:, None, :]
@@ -180,16 +269,20 @@
     shaping = prototype(TAPS, length)
     beam_total = beam_dir.shape[0]
     beam_dev = beam_total // group_count
-    rows_dev = RADIX // section_count
-    rows_piece = rows_dev // PIECES
-    chans_own = rows_piece * RADIX // group_count
+    highs_dev = RADIX // section_count
+    rows_piece = RADIX // PIECES
+    chans_piece = highs_dev * rows_piece
+    chans_own = chans_piece // group_count
 
     loading = jnp.exp2(load_exp.astype(jnp.float32))
-    loading = lax.all_gather(loading, ("section", "gx"), tiled=True)
-    loading = jnp.transpose(loading.reshape(RADIX, RADIX))
-    loading = lax.dynamic_slice_in_dim(loading, section * rows_dev, rows_dev, 0)
-    loading = loading.reshape(PIECES, group_count, chans_own)
-    loading = lax.dynamic_index_in_dim(loading, group, 1, keepdims=False)
+    if highs_dev % group_count == 0:
+        loading = loading.reshape(-1, PIECES, rows_piece)
+    else:
+        loading = lax.all_gather(loading, ("section", "gx"), tiled=True)
+        loading = loading.reshape(section_count, highs_dev, PIECES, rows_piece)[section]
+        loading = jnp.transpose(loading, (1, 0, 2)).reshape(PIECES, group_count, chans_own)
+        loading = jnp.transpose(loading[:, group].reshape(PIECES, 1, chans_own), (1, 0, 2))
+    loading = jnp.transpose(loading, (1, 0, 2)).reshape(PIECES * chans_own)
 
     angle_beam = math.pi / beam_total * (beam_dir.astype(jnp.float32) + 0.5) - 0.5 * math.pi
     mine = lax.dynamic_slice_in_dim(positions, group * inputs_dev, inputs_dev, 1)
@@ -197,41 +290,40 @@
         jnp.sin(angle_beam)[:, None] * mine[0][None, :]
         + jnp.cos(angle_beam)[:, None] * mine[1][None, :]
     )
-    rows = (section * rows_dev + jnp.arange(rows_dev, dtype=jnp.int32)).astype(jnp.float32)
+    rows = jnp.arange(RADIX, dtype=jnp.int32).astype(jnp.float32)
     low_cos, low_sin = rotation(2.0 * math.pi * (0.75 + 0.5 * rows / length), delay)
-    steps = jnp.arange(RADIX, dtype=jnp.int32).astype(jnp.float32)
+    steps = (section * highs_dev + jnp.arange(highs_dev, dtype=jnp.int32)).astype(jnp.float32)
     high_cos, high_sin = rotation(math.pi * RADIX / length * steps, delay)
-
-    turned = first_stage(halo_filter(samples))
-    turned = turned.reshape(
-        block_dev, section_count, rows_dev, 2 * RADIX, inputs_dev
-    )
-    formed = []
-    for piece in range(PIECES):
+    high_cos, high_sin = high_cos[:, None], high_sin[:, None]
+
+    projections, grams = [], []
+    for piece, spectra in enumerate(analysis(samples, section_count)):
         span = slice(piece * rows_piece, (piece + 1) * rows_piece)
-        part = turned[:, :, span].reshape(
-            block_dev, section_count * rows_piece, 2 * RADIX, inputs_dev
+        spectra = lax.all_to_all(spectra, "section", split_axis=0, concat_axis=0, tiled=True)
+        spectra = spectra.reshape(snapshots, rows_piece, 2, highs_dev, inputs_dev)
+        spectra = jnp.transpose(spectra, (3, 1, 2, 0, 4)).reshape(
+            chans_piece, 2, snapshots, inputs_dev
         )
-        spectra = second_stage(part).reshape(
-            block_dev, section_count, rows_piece, 2, RADIX, inputs_dev
-        )
-        spectra = jnp.transpose(spectra, (1, 0, 2, 3, 4, 5))
-        spectra = lax.all_to_all(spectra, "section", split_axis=0, concat_axis=0, tiled=True)
-        spectra = spectra.reshape(snapshots, rows_piece, 2, RADIX, inputs_dev)
-        spectra = jnp.transpose(spectra, (1, 3, 2, 0, 4)).reshape(
-            rows_piece * RADIX, 2, snapshots, inputs_dev
-        )
-        lc, ls = low_cos[span][:, None], low_sin[span][:, None]
+        lc, ls = low_cos[span], low_sin[span]
         steer = jnp.concatenate(
             [lc * high_cos - ls * high_sin, lc * high_sin + ls * high_cos], axis=-1
         ).astype(jnp.bfloat16)
-        steer = steer.reshape(rows_piece * RADIX, beam_total, 2 * inputs_dev)
+        steer = steer.reshape(chans_piece, beam_total, 2 * inputs_dev)
         projected, packed = local_products(spectra, steer)
-        projected = lax.psum_scatter(projected, "gx", scatter_dimension=0, tiled=True)
-        packed = lax.psum_scatter(packed, "gx", scatter_dimension=0, tiled=True)
-        formed.append(solve(projected, packed, loading[piece], inputs_all))
-
-    beam_spec = jnp.stack(formed, axis=1)
+        projections.append(
+            lax.psum_scatter(
+                projected.reshape(chans_piece, -1), "gx", scatter_dimension=0, tiled=True
+            )
+        )
+        grams.append(packed.reshape(group_count, chans_own, -1))
+    packed = jnp.concatenate(grams, axis=1).reshape(group_count * PIECES * chans_own, -1)
+    packed = lax.psum_scatter(packed, "gx", scatter_dimension=0, tiled=True)
+    beam_spec = solve(
+        jnp.concatenate(projections, axis=0).reshape(-1, beam_total, 2 * snapshots),
+        packed.reshape(-1, snapshots, snapshots),
+        loading,
+        inputs_all,
+    )
     shaped = beam_spec.reshape(
         2, PIECES, chans_own, group_count, beam_dev, section_count, block_dev
     )
@@ -248,8 +340,8 @@
     opened = returned.reshape(
         2, group_count, beam_dev, section_count, block_dev, PIECES, chans_own
     )
-    by_beam = jnp.transpose(opened, (0, 2, 4, 3, 5, 1, 6)).reshape(
-        2, beam_dev, block_dev, RADIX, RADIX
+    by_beam = jnp.transpose(opened, (0, 2, 4, 5, 3, 1, 6)).reshape(
+        2, beam_dev, block_dev, PIECES, RADIX, rows_piece
     )
     series = synthesis_transform(by_beam).astype(jnp.float32)
     margin_zeros = jnp.zeros((2, beam_dev, history, length), jnp.float32)

time: 1390 us -> 937 us (0.67)
  waiting for transfers between devices: 770 us -> 326 us
  Pallas kernels: 0 us -> 88.1 us
  local copies, waits for them, and re-layouts: 262 us -> 187 us
  blocking collectives: 90.4 us -> 125 us
  matrix products: 97.3 us -> 72.8 us
  other arithmetic: 115 us -> 93.9 us
  starting transfers between devices: 37.1 us -> 19.8 us
    reduce_scatter x4 -> x0, waiting for transfers between devices: 344 us -> none  [body(): lax.psum_scatter(projected, 'gx', scatter_dimension=0, tiled=True)]
    reduce_scatter x4 -> x1, waiting for transfers between devices: 197 us -> 0.02 us  [body(): packed = lax.psum_scatter(packed, 'gx', scatter_dimension=0, tiled=True)]
    unnamed x8 -> x5, waiting for transfers between devices: 0.8 us -> 170 us
    all_to_all x0 -> x1, blocking collectives: none -> 96.3 us  [body(): lax.all_to_all(spectra, 'section', split_axis=0, concat_axis=0, tiled=True)]
    pallas_call x0 -> x1, Pallas kernels: none -> 88.1 us  [analysis(): pl.pallas_call(lambda *refs: analysis_kernel(parts, *refs), grid=(blocks,...]
    all_to_all x4 -> x1, waiting for transfers between devices: 141 us -> 70 us  [body(): lax.all_to_all(spectra, 'section', split_axis=0, concat_axis=0, tiled=True)]
    all_gather x1 -> x0, blocking collectives: 61.7 us -> none  [body(): loading = lax.all_gather(loading, ('section', 'gx'), tiled=True)]
    convert_element_type x2 -> x0, other arithmetic: 34.6 us -> none  [the longest x1 20.6 us: halo_filter(): return filtered.astype(jnp.bfloat16)]
  transfers between devices with their start and end apart: 15 -> 7, of which waited for: 14 -> 6; matrix products, arithmetic and copies ran while one was open for 12% -> 13% of each run, Pallas kernels for 0% -> 0%
where the time goes in v3:
time: 937 us; the launch traced here: 927 us
  waiting for transfers between devices  326 us (35%)
  local copies, waits for them, and re-layouts  187 us (20%)
  blocking collectives  125 us (13%)
  other arithmetic  93.9 us (10%)
  Pallas kernels  88.1 us (9%)
  matrix products  72.8 us (8%)
  starting transfers between devices  19.8 us (2%)
  between operations  13.8 us (1%)
    unnamed x5, waiting for transfers between devices  170 us
    all_to_all x1, blocking collectives, body(): lax.all_to_all(spectra, 'section', split_axis=0, concat_axis=0, tiled=True)  96.3 us
    pallas_call x1, Pallas kernels, analysis(): pl.pallas_call(lambda *refs: analysis_kernel(parts, *refs), grid=(blocks,...  88.1 us
    ppermute x2, waiting for transfers between devices, from_behind(): lax.ppermute(value, axis, [(source, source + steps) for source in range(i...  72.2 us
    all_to_all x1, waiting for transfers between devices, body(): lax.all_to_all(spectra, 'section', split_axis=0, concat_axis=0, tiled=True)  70 us
    unnamed x36, local copies, waits for them, and re-layouts  45.2 us
    dot_general x2, matrix products, local_products(): jnp.einsum('fbm,fkm->fbk', steer, blocked, preferred_element_type=jnp.flo...  32 us
    dot_general x2, matrix products, local_products(): jnp.einsum('fqm,fkm->fqk', upper, blocked, preferred_element_type=jnp.flo...  29.7 us
  transfers between devices with their start and end apart: 7, of which 6 were waited for; matrix products, arithmetic and copies ran while one was open for 13% of the time, Pallas kernels for 0%

profile of v3, /device:TPU:1, one launch (start us, length us, event | category | flops | bytes accessed | tf_op | source)
XLA Modules:
  0.0 926.6 jit_solution(17798345829179646436)
XLA Ops:
  6.5 22.5 %copy.61 = bf16[2,128,8,4096]{1,3,0,2:T(8,128)(2,1)} copy(bf16[2,128,8,4096]{3,2,1,0:T(8,128)(2,1)} %param.5) | data formatting | bytes 33554432 | tf_op args[0]
  29.0 5.8 slice.131
  34.9 4.5 collective-permute-start
  41.5 66.1 %collective-permute-done = bf16[3,2,4096,128]{3,2,1,0:T(8,128)(2,1)} collective-permute-done((bf16[3,2,4096,128]{3,2,1,0:T(8,128)(2,1)}, bf16[3,2,4096,128]{3,2,1,0:T(8,128)(2,1)}, u32[]{:S(2)}, u32[]{:S(2)}) %collective-permute-start) | collective-permute-done | bytes 6291488 | tf_op jit(solution)/shard_map/ppermute | solution.py:19
  107.6 19.7 %pad_maximum_fusion.refs_0_.refs_1_.refs_2_.refs_3_ = bf16[11,2,4096,128]{3,2,1,0:T(8,128)(2,1)} fusion(bf16[8,2,4096,128]{3,2,1,0:T(8,128)(2,1)} %bitcast.85, bf16[3,2,4096,128]{3,2,1,0:T(8,128)(2,1)} %collective-permute-done), kind=kLoop, calls=%fused_computation | loop fusion | flops 11534336 | bytes 46137344 | tf_op jit(solution)/shard_map/concatenate | solution.py:60
  127.3 5.1 broadcast_in_dim.33.refs_4_
  136.2 88.1 %shard_map.46 = (bf16[4,8,32,32,128]{4,3,2,1,0:T(8,128)(2,1)}, bf16[4,8,32,32,128]{4,3,2,1,0:T(8,128)(2,1)}) custom-call(bf16[11,2,4096,128]{3,2,1,0:T(8,128)(2,1)} %pad_maximum_fusion.refs_0_.refs_1_.refs_2_.refs_3_, bf16[11,2,4096,128]{3,2,1,0:T(8,128)(2,1)} %pad_maximum_fusion.refs_0_.refs_1_.refs_2_.refs_3_, ...), custom_call_target="tpu_custom_call" | custom-call | flops 4294967296 | bytes 83886080 | tf_op jit(solution)/shard_map/pallas_call | solution.py:138
  224.3 96.3 %all_to_all.20 = bf16[4,8,32,32,128]{4,3,2,1,0:T(8,128)(2,1)} all-to-all(bf16[4,8,32,32,128]{4,3,2,1,0:T(8,128)(2,1)} %get-tuple-element.9), channel_id=1, replica_groups=mesh['section'=4,'gx'=8] {'section'}, dimensions={0} | all-to-all | bytes 16777216 | tf_op jit(solution)/shard_map/all_to_all | solution.py:302
  320.7 6.7 all-to-all-start
  327.3 12.0 %copy.65 = bf16[16,32,2,32,128]{4,3,1,0,2:T(8,128)(2,1)} copy(bf16[16,32,2,32,128]{4,0,2,1,3:T(8,128)(2,1)} %bitcast.90) | data formatting | bytes 16777216 | tf_op jit(solution)/shard_map/transpose | solution.py:304
  339.4 5.0 fusion.83
  345.5 4.2 slice_bitcast_fusion
  349.7 70.0 %all-to-all-done = bf16[4,8,32,32,128]{4,3,2,1,0:T(8,128)(2,1)} async-done(((bf16[4,8,32,32,128]{4,3,2,1,0:T(8,128)(2,1)}), bf16[4,8,32,32,128]{4,3,2,1,0:T(8,128)(2,1)}, u32[]{:S(2)}, u32[]{:S(2)}) %all-to-all-start) | async-done | bytes 8388640 | tf_op jit(solution)/shard_map/all_to_all | solution.py:302
  419.7 12.0 %copy.63 = bf16[16,32,2,32,128]{4,3,1,0,2:T(8,128)(2,1)} copy(bf16[16,32,2,32,128]{4,0,2,1,3:T(8,128)(2,1)} %bitcast.9) | data formatting | bytes 16777216 | tf_op jit(solution)/shard_map/transpose | solution.py:304
  431.7 7.6 slice_bitcast_fusion.2
  442.9 15.0 %fusion.12 = f32[512,32,64]{2,1,0:T(8,128)} fusion(bf16[512,32,128]{2,1,0:T(8,128)(2,1)} %get-tuple-element.16, bf16[512,32,128]{2,1,0:T(8,128)(2,1)} %get-tuple-element.17, bf16[512,32,128]{2,1,0:T(8,128)(2,1)} %fusion.83), kind=kOutput, calls=%fused_computation.21 | convolution fusion | flops 620756992 | bytes 16777216 | tf_op jit(solution)/shard_map/fqm,fkm->fqk/dot_general | solution.py:189
  458.0 14.7 %fusion.8 = f32[512,32,64]{2,1,0:T(8,128)} fusion(bf16[512,32,128]{2,1,0:T(8,128)(2,1)} %get-tuple-element.14, bf16[512,32,128]{2,1,0:T(8,128)(2,1)} %get-tuple-element.15, bf16[512,32,128]{2,1,0:T(8,128)(2,1)} %fusion.82), kind=kOutput, calls=%fused_computation.17 | convolution fusion | flops 620756992 | bytes 16777216 | tf_op jit(solution)/shard_map/fqm,fkm->fqk/dot_general | solution.py:189
  472.6 19.7 %slice_select_fusion.1 = (f32[512,32,32]{2,1,0:T(8,128)}, f32[512,32,32]{2,1,0:T(8,128)}) fusion(f32[512,32,64]{2,1,0:T(8,128)} %fusion.8, pred[32,32]{1,0:T(8,128)(4,1)S(1)} %iota_compare_fusion.2, f32[512,32,64]{2,1,0:T(8,128)} %fusion.12), kind=kLoop, calls=%fused_computation.16 | loop fusion | flops 1048576 | bytes 12583936 | tf_op jit(solution)/shard_map/jit(_where)/select_n | solution.py:192
  492.3 6.6 reshape.418
  499.0 2.8 copy.84
  501.8 6.6 reshape.419
  508.4 2.8 copy.85
  511.2 4.6 pad_maximum_fusion.1
  515.8 3.0 copy.101
  521.5 7.4 multiply_cosine_fusion
  529.3 13.9 %subtract_convert_fusion.1 = (bf16[16,32,64,128]{3,2,1,0:T(8,128)(2,1)}, bf16[16,32,64,128]{3,2,1,0:T(8,128)(2,1)}, bf16[16,32,64,128]{3,2,1,0:T(8,128)(2,1)}, bf16[16,32,64,128]{3,2,1,0:T(8,128)(2,1)}) fusion(f32[16,64,128]{2,1,0:T(8,128)S(1)} %get-tuple-element.44, f32[32,64,128]{2,1,0:T(8,128)S(1)} %get-tuple-element.54, ...), kind=kLoop, calls=%fused_computation.14 | loop fusion | flops 67108864 | bytes 38797312 | tf_op jit(solution)/shard_map/convert.18
  543.1 15.9 %fusion.19 = bf16[512,64,64]{2,1,0:T(8,128)(2,1)} fusion(bf16[512,64,128]{2,1,0:T(8,128)(2,1)} %bitcast.101, bf16[512,64,128]{2,1,0:T(8,128)(2,1)} %bitcast.100, bf16[512,32,128]{2,1,0:T(8,128)(2,1)} %get-tuple-element.15, bf16[512,32,128]{2,1,0:T(8,128)(2,1)} %fusion.82, bf16[512,32,128]{2,1,0:T(8,128)(2,1)} %get-tuple-element.14), kind=kOutput, calls=%fused_computation.26 | convolution fusion | flops 1176502272 | bytes 33554432 | tf_op jit(solution)/shard_map/fbm,fkm->fbk/dot_general | solution.py:188
  559.0 9.8 %copy.64 = bf16[512,64,64]{0,2,1:T(8,128)(2,1)} copy(bf16[512,64,64]{2,1,0:T(8,128)(2,1)} %fusion.19) | data formatting | bytes 8388608 | tf_op jit(solution)/shard_map/convert_element_type | solution.py:193
  568.8 6.4 copy.88
  575.3 16.1 %fusion.16 = bf16[512,64,64]{2,1,0:T(8,128)(2,1)} fusion(bf16[512,64,128]{2,1,0:T(8,128)(2,1)} %bitcast.98, bf16[512,64,128]{2,1,0:T(8,128)(2,1)} %bitcast.99, bf16[512,32,128]{2,1,0:T(8,128)(2,1)} %get-tuple-element.17, bf16[512,32,128]{2,1,0:T(8,128)(2,1)} %fusion.83, bf16[512,32,128]{2,1,0:T(8,128)(2,1)} %get-tuple-element.16), kind=kOutput, calls=%fused_computation.25 | convolution fusion | flops 1176502272 | bytes 33554432 | tf_op jit(solution)/shard_map/fbm,fkm->fbk/dot_general | solution.py:188
  591.5 9.8 %copy.66 = bf16[512,64,64]{0,2,1:T(8,128)(2,1)} copy(bf16[512,64,64]{2,1,0:T(8,128)(2,1)} %fusion.16) | data formatting | bytes 8388608 | tf_op jit(solution)/shard_map/convert_element_type | solution.py:193
  601.3 6.4 copy.90
  610.4 4.5 copy.71
  614.8 4.5 copy.72
  619.4 80.4 %reduce-scatter.10.cloned.1.call-done = bf16[64,4096]{1,0:T(8,128)(2,1)} async-done(((bf16[512,4096]{1,0:T(8,128)(2,1)}), bf16[64,4096]{1,0:T(8,128)(2,1)}) %reduce-scatter.10.cloned.1.call-update) | async-done | bytes 524304
  701.3 90.0 %reduce-scatter.12.cloned.1.call-done = bf16[64,4096]{1,0:T(8,128)(2,1)} async-done(((bf16[512,4096]{1,0:T(8,128)(2,1)}), bf16[64,4096]{1,0:T(8,128)(2,1)}) %reduce-scatter.12.cloned.1.call-update) | async-done | bytes 524304
  793.4 3.8 copy.73
  797.2 9.8 %fusion.25 = f32[128,64,64]{1,2,0:T(8,128)} fusion(bf16[128,64,64]{2,1,0:T(8,128)(2,1)} %copy.73, f32[128,32,64]{1,2,0:T(8,128)} %copy.72, f32[128,32,64]{1,2,0:T(8,128)} %copy.71), kind=kOutput, calls=%fused_computation.38 | convolution fusion | flops 403177472 | bytes 5242880 | tf_op jit(solution)/shard_map/fbq,fqk->fbk/dot_general | solution.py:211
  807.0 4.7 copy.74
  818.1 4.7 maximum_bitcast_fusion
  824.5 28.8 %all_to_all.21 = bf16[2,8,8,4,1024]{4,2,3,0,1:T(8,128)(2,1)S(1)} all-to-all(bf16[2,8,8,4,1024]{4,2,3,0,1:T(8,128)(2,1)S(1)} %copy.78), channel_id=1, replica_groups=mesh['section'=4,'gx'=8] {'gx'}, dimensions={1} | all-to-all | bytes 2097152 | tf_op jit(solution)/shard_map/all_to_all | solution.py:334
  854.4 5.6 all-to-all-start.3
  860.5 13.1 %all-to-all-done.3 = bf16[2,8,8,4,1024]{4,2,1,0,3:T(8,128)(2,1)S(1)} async-done(((bf16[2,8,8,4,1024]{4,2,1,0,3:T(8,128)(2,1)}), bf16[2,8,8,4,1024]{4,2,1,0,3:T(8,128)(2,1)S(1)}, u32[]{:S(2)}, u32[]{:S(2)}) %all-to-all-start.3) | async-done | bytes 1048608 | tf_op jit(solution)/shard_map/all_to_all | solution.py:333
  875.9 4.0 copy.103
  879.9 3.3 reshape_reshape.3
  883.2 5.5 copy.81
  901.4 4.2 reshape.416
  912.4 6.1 collective-permute-done.1
  (100 shorter events, 52.7 us)
Async XLA Ops:
  6.5 512.6 %copy-start = (f32[2,1024]{1,0:T(2,128)S(1)}, f32[2,1024]{1,0:T(2,128)}, u32[]{:S(2)}) copy-start(f32[2,1024]{1,0:T(2,128)} %param.6) | copy-start | bytes 24580
  34.9 72.7 %collective-permute-start = (bf16[3,2,4096,128]{3,2,1,0:T(8,128)(2,1)}, bf16[3,2,4096,128]{3,2,1,0:T(8,128)(2,1)}, u32[]{:S(2)}, u32[]{:S(2)}) collective-permute-start(bf16[3,2,4096,128]{3,2,1,0:T(8,128)(2,1)} %slice.131), channel_id=1, source_target_pairs={{0,8},{8,16},{16,24},{1,9},{9,17},{17,25},{2,10},{10,18},{18,26},{... | collective-permute-start | bytes 18874376 | tf_op jit(solution)/shard_map/ppermute | solution.py:19
  39.7 0.6 copy-start.11
  39.8 87.5 %copy-start.10 = (bf16[128,128]{1,0:T(8,128)(2,1)}, bf16[128,128]{1,0:T(8,128)(2,1)S(1)}, u32[]{:S(2)}) copy-start(bf16[128,128]{1,0:T(8,128)(2,1)S(1)} %fusion.57.refs_5_) | copy-start | bytes 98308
  41.2 86.1 %copy-start.6 = (f32[16384]{0:T(1024)}, f32[16384]{0:T(1024)S(1)}, u32[]{:S(2)}) copy-start(f32[16384]{0:T(1024)S(1)} %fusion.47) | copy-start | bytes 196612
  41.4 91.0 %copy-start.8 = (f32[64,64]{1,0:T(8,128)}, f32[64,64]{1,0:T(8,128)S(1)}, u32[]{:S(2)}) copy-start(f32[64,64]{1,0:T(8,128)S(1)} %fusion.63) | copy-start | bytes 49156
  320.7 99.0 %all-to-all-start = ((bf16[4,8,32,32,128]{4,3,2,1,0:T(8,128)(2,1)}), bf16[4,8,32,32,128]{4,3,2,1,0:T(8,128)(2,1)}, u32[]{:S(2)}, u32[]{:S(2)}) async-start(bf16[4,8,32,32,128]{4,3,2,1,0:T(8,128)(2,1)} %get-tuple-element.8), calls=%async_computation | async-start | bytes 16777216 | tf_op jit(solution)/shard_map/all_to_all | solution.py:302
  327.3 281.3 %reduce-scatter.8.cloned.1.call-start = ((), (), s32[]{:S(2)}) async-start(), calls=%async_computation.7 | async-start | bytes 4718592 | tf_op jit(solution)/shard_map/reduce_scatter | solution.py:320
  339.4 6.2 copy-start.2
  431.7 8.8 copy-start.3
  518.8 0.7 copy-start.13
  518.9 180.9 %reduce-scatter.10.cloned.1.call-start = ((), (), s32[]{:S(2)}) async-start(), calls=%async_computation.8 | async-start | bytes 4718592
  575.3 216.0 %reduce-scatter.12.cloned.1.call-start = ((), (), s32[]{:S(2)}) async-start(), calls=%async_computation.9 | async-start | bytes 4718592
  607.7 0.7 copy-start.14
  792.8 4.4 copy-start.4
  811.7 2.5 copy-start.5
  824.1 36.3 %copy-start.7 = (f32[16384]{0:T(1024)S(1)}, f32[16384]{0:T(1024)}, u32[]{:S(2)}) copy-start(f32[16384]{0:T(1024)} %copy-done.6) | copy-start | bytes 196612
  854.4 19.2 %all-to-all-start.3 = ((bf16[2,8,8,4,1024]{4,2,1,0,3:T(8,128)(2,1)}), bf16[2,8,8,4,1024]{4,2,1,0,3:T(8,128)(2,1)S(1)}, u32[]{:S(2)}, u32[]{:S(2)}) async-start(bf16[2,8,8,4,1024]{4,2,1,0,3:T(8,128)(2,1)} %copy.79), calls=%async_computation.4 | async-start | bytes 2097152 | tf_op jit(solution)/shard_map/all_to_all | solution.py:333
  883.2 6.5 copy-start.12
  891.3 4.2 copy-start.9
  907.7 12.1 %copy-start.1 = (f32[2,1024]{1,0:T(2,128)S(1)}, f32[2,1024]{1,0:T(2,128)}, u32[]{:S(2)}) copy-start(f32[2,1024]{1,0:T(2,128)} %param.6) | copy-start | bytes 24580
  909.7 8.8 collective-permute-start.1
Sparse Core Ops, SparseCore 0:
  519.0 89.0 reduce-scatter.7
  612.1 87.6 reduce-scatter.9
  703.4 87.7 reduce-scatter.11
